TPU v7x, 32 devices: a whole 2x2x4 slice. The times are simulated.
32 devices in a mesh: shard: 4 (over x, core), ctx: 8 (over z, y).
Axes of the slice: x: 2, y: 2, z: 4, core: 2. Of those that a mesh axis runs over, the one named last changes fastest.
Arguments:
- inputs: bfloat16 [8, 1024, 512], P('shard', 'ctx'), may hold values from -6 to 6
- memory: bfloat16 [8, 20, 512], P('shard'), may hold values from -6 to 6
- lengths: int32 [8], P('shard'), may hold values from 128 to 1024, as said below
- w_query: bfloat16 [512, 512], P('shard'), may hold values from -0.25 to 0.25
- w_key: bfloat16 [512, 512], P('shard'), may hold values from -0.25 to 0.25
- w_value: bfloat16 [512, 512], P('shard'), may hold values from -0.25 to 0.25
- w_out: bfloat16 [512, 512], P('shard'), may hold values from -6 to 6
- w_up: bfloat16 [512, 2048], P('shard'), may hold values from -0.25 to 0.25
- w_down: bfloat16 [2048, 512], P('shard'), may hold values from -0.125 to 0.125
- b_query: bfloat16 [512], P('shard'), may hold values from -3 to 3
- b_value: bfloat16 [512], P('shard'), may hold values from -0.0625 to 0.0625
- b_out: bfloat16 [512], P('shard'), may hold values from -3 to 3
- b_up: bfloat16 [2048], P('shard'), may hold values from -3 to 3
- b_down: bfloat16 [512], P('shard'), may hold values from -3 to 3
- first_gain: bfloat16 [512], P('shard'), may hold values from 0.5 to 1.5
- first_bias: bfloat16 [512], P('shard'), may hold values from -3 to 3
- second_gain: bfloat16 [512], P('shard'), may hold values from 0.5 to 1.5
- second_bias: bfloat16 [512], P('shard'), may hold values from -3 to 3
- out_grad: bfloat16 [8, 1024, 512], P('shard', 'ctx'), may hold values from -6 to 6
Outputs:
- layer_out: bfloat16 [8, 1024, 512], P('shard', 'ctx')
- input_grad: float32 [8, 1024, 512], P('shard', 'ctx')
- memory_grad: float32 [8, 20, 512], P('shard')
- grad_w_query: float32 [512, 512], P('shard')
- grad_w_key: float32 [512, 512], P('shard')
- grad_w_value: float32 [512, 512], P('shard')
- grad_w_out: float32 [512, 512], P('shard')
- grad_w_up: float32 [512, 2048], P('shard')
- grad_w_down: float32 [2048, 512], P('shard')
- grad_b_query: float32 [512], P('shard')
- grad_b_value: float32 [512], P('shard')
- grad_b_out: float32 [512], P('shard')
- grad_b_up: float32 [2048], P('shard')
- grad_b_down: float32 [512], P('shard')
- grad_first_gain: float32 [512], P('shard')
- grad_first_bias: float32 [512], P('shard')
- grad_second_gain: float32 [512], P('shard')
- grad_second_bias: float32 [512], P('shard')
- stream_rms: float32 [8, 3], P('shard')
Inputs may be any that keep to these rules, and one draw needn't show every extreme that they name: `lengths`: in every draw one sequence is 1024 tokens long.
All inputs are finite; a program needn't handle non-finite values.
Results may differ from a plain program's by a relative error of at most 0.02.
Values may be sent and summed in bfloat16 or wider, within the bound.
A program may use at most 192 MiB of HBM per device.

v0:
```python
import math

import jax
import jax.numpy as jnp
from jax import lax
from jax.sharding import PartitionSpec as P

HEADS = 8
HEAD_DIM = 64


eps = 1e-05


def matmul(operand, second):
    return jnp.dot(operand, second, preferred_element_type=jnp.float32)


def outer_sum(operand, second):
    return lax.dot_general(
        operand, second, (((0,), (0,)), ((), ())), preferred_element_type=jnp.float32
    )


def back_product(operand, second):
    return lax.dot_general(
        operand, second, (((1,), (1,)), ((), ())), preferred_element_type=jnp.float32
    )


def to_float(tensor):
    return tensor.astype(jnp.float32)


def smooth_act(values):
    return jax.nn.gelu(values, approximate=True)


def split_heads(tensor):
    return tensor.reshape(tensor.shape[0], tensor.shape[1], HEADS, HEAD_DIM)


def head_scores(queries, key_heads):
    return jnp.einsum(
        "sqhd,skhd->sqhk", queries, key_heads, preferred_element_type=jnp.float32
    ) * HEAD_DIM ** (-0.5)


def norm_forward(matrix, gain, offset):
    row_mean = jnp.mean(matrix, axis=-1, keepdims=True)
    centered = matrix - row_mean
    inverse = lax.rsqrt(jnp.mean(centered * centered, axis=-1, keepdims=True) + eps)
    unit_rows = centered * inverse
    return (unit_rows * gain + offset, unit_rows, inverse)


def norm_backward(cotangent, unit_rows, inverse, gain):
    scaled = cotangent * gain
    centered_grad = (
        scaled
        - jnp.mean(scaled, axis=-1, keepdims=True)
        - unit_rows * jnp.mean(scaled * unit_rows, axis=-1, keepdims=True)
    )
    return (
        inverse * centered_grad,
        jnp.sum(cotangent * unit_rows, axis=0),
        jnp.sum(cotangent, axis=0),
    )


def in_blocks(update, carried, arrays, first_row, slice_dim):
    piece_rows = arrays[0].shape[slice_dim]
    block_len = math.gcd(piece_rows, 1024)
    if block_len == piece_rows:
        return update(carried, arrays, first_row)

    def one_block(current, number):
        block_start = number * block_len
        sliced = tuple(
            (
                lax.dynamic_slice_in_dim(tensor, block_start, block_len, slice_dim)
                for tensor in arrays
            )
        )
        return (update(current, sliced, first_row + block_start), None)

    carried, unused = lax.scan(
        one_block, carried, jnp.arange(piece_rows // block_len, dtype=jnp.int32)
    )
    return carried


def softmax_update(carried, pieces, first_row, queries, lengths):
    row_max, row_total, weighted = carried
    key_piece, value_piece = pieces
    piece_rows = key_piece.shape[1]
    scores = head_scores(queries, split_heads(key_piece))
    key_mask = (first_row + jnp.arange(piece_rows, dtype=jnp.int32))[None, :] < lengths[:, None]
    scores = jnp.where(key_mask[:, None, None, :], scores, -1e30)
    new_max = jnp.maximum(row_max, jnp.max(scores, axis=-1))
    factor = jnp.exp(row_max - new_max)
    exponent = jnp.exp(scores - new_max[..., None])
    row_total = row_total * factor + jnp.sum(exponent, axis=-1)
    weighted = weighted * factor[..., None] + jnp.einsum(
        "sqhk,skhd->sqhd",
        exponent.astype(jnp.bfloat16),
        split_heads(value_piece),
        preferred_element_type=jnp.float32,
    )
    return (new_max, row_total, weighted)


def query_update(grad_q, pieces, first_row, queries, grad_heads, log_total, row_delta, lengths):
    key_piece, value_piece = pieces
    piece_rows = key_piece.shape[1]
    key_heads = split_heads(key_piece)
    scores = head_scores(queries, key_heads)
    key_mask = (first_row + jnp.arange(piece_rows, dtype=jnp.int32))[None, :] < lengths[:, None]
    scores = jnp.where(key_mask[:, None, None, :], scores, -1e30)
    attn_probs = jnp.exp(scores - log_total[..., None])
    value_dots = jnp.einsum(
        "sqhd,skhd->sqhk", grad_heads, split_heads(value_piece), preferred_element_type=jnp.float32
    )
    d_scores = (attn_probs * (value_dots - row_delta[..., None])).astype(jnp.bfloat16)
    return grad_q + jnp.einsum(
        "sqhk,skhd->sqhd", d_scores, key_heads, preferred_element_type=jnp.float32
    ) * HEAD_DIM ** (-0.5)


def key_update(carried, pieces, first_row, key_heads, value_heads, log_all, delta_all, key_mask):
    grad_k, grad_v = carried
    query_piece, grad_piece = pieces
    piece_rows = query_piece.shape[1]
    log_total = lax.dynamic_slice_in_dim(log_all, first_row, piece_rows, 1)
    row_delta = lax.dynamic_slice_in_dim(delta_all, first_row, piece_rows, 1)
    queries = split_heads(query_piece)
    grad_heads = split_heads(grad_piece)
    scores = head_scores(queries, key_heads)
    scores = jnp.where(key_mask[:, None, None, :], scores, -1e30)
    attn_probs = jnp.exp(scores - log_total[..., None])
    grad_v = grad_v + jnp.einsum(
        "sqhk,sqhd->skhd",
        attn_probs.astype(jnp.bfloat16),
        grad_heads,
        preferred_element_type=jnp.float32,
    )
    value_dots = jnp.einsum(
        "sqhd,skhd->sqhk", grad_heads, value_heads, preferred_element_type=jnp.float32
    )
    d_scores = (attn_probs * (value_dots - row_delta[..., None])).astype(jnp.bfloat16)
    grad_k = grad_k + jnp.einsum(
        "sqhk,sqhd->skhd", d_scores, queries, preferred_element_type=jnp.float32
    ) * HEAD_DIM ** (-0.5)
    return (grad_k, grad_v)


def local(
    inputs,
    memory,
    lengths,
    w_query,
    w_key,
    w_value,
    w_out,
    w_up,
    w_down,
    b_query,
    b_value,
    b_out,
    b_up,
    b_down,
    first_gain,
    first_bias,
    second_gain,
    second_bias,
    out_grad,
):
    gathered = (
        lax.all_gather(w_query, "shard", axis=0, tiled=True),
        lax.all_gather(w_key, "shard", axis=0, tiled=True),
        lax.all_gather(w_value, "shard", axis=0, tiled=True),
        lax.all_gather(w_out, "shard", axis=0, tiled=True),
        lax.all_gather(w_up, "shard", axis=0, tiled=True),
        lax.all_gather(w_down, "shard", axis=0, tiled=True),
        lax.all_gather(b_query, "shard", axis=0, tiled=True),
        lax.all_gather(b_value, "shard", axis=0, tiled=True),
        lax.all_gather(b_out, "shard", axis=0, tiled=True),
        lax.all_gather(b_up, "shard", axis=0, tiled=True),
        lax.all_gather(b_down, "shard", axis=0, tiled=True),
        lax.all_gather(first_gain, "shard", axis=0, tiled=True),
        lax.all_gather(first_bias, "shard", axis=0, tiled=True),
        lax.all_gather(second_gain, "shard", axis=0, tiled=True),
        lax.all_gather(second_bias, "shard", axis=0, tiled=True),
    )
    (
        full_query,
        full_key,
        full_value,
        full_out,
        full_up,
        full_down,
        bias_query,
        bias_value,
        bias_out,
        bias_up,
        bias_down,
        gain_one,
        offset_one,
        gain_two,
        offset_two,
    ) = gathered
    seq_count, local_len, features = inputs.shape
    mem_rows = memory.shape[1]
    token_rows = inputs.reshape(seq_count * local_len, features)
    mem_flat = memory.reshape(seq_count * mem_rows, features)
    query = (
        (matmul(token_rows, full_query) + to_float(bias_query))
        .astype(jnp.bfloat16)
        .reshape(seq_count, local_len, features)
    )
    key = matmul(token_rows, full_key).astype(jnp.bfloat16).reshape(seq_count, local_len, features)
    value = (
        (matmul(token_rows, full_value) + to_float(bias_value))
        .astype(jnp.bfloat16)
        .reshape(seq_count, local_len, features)
    )
    mem_key = matmul(mem_flat, full_key).astype(jnp.bfloat16).reshape(seq_count, mem_rows, features)
    mem_value = (
        (matmul(mem_flat, full_value) + to_float(bias_value))
        .astype(jnp.bfloat16)
        .reshape(seq_count, mem_rows, features)
    )
    query_heads = split_heads(query)
    mem_key_heads = split_heads(mem_key)
    mem_value_heads = split_heads(mem_value)
    position_zero = lax.axis_index("ctx") * local_len
    key_mask = (position_zero + jnp.arange(local_len, dtype=jnp.int32))[None, :] < lengths[:, None]
    mem_scores = head_scores(query_heads, mem_key_heads)
    mem_max = jnp.max(mem_scores, axis=-1)
    mem_exponent = jnp.exp(mem_scores - mem_max[..., None])
    start_state = (
        mem_max,
        jnp.sum(mem_exponent, axis=-1),
        jnp.einsum(
            "sqhk,skhd->sqhd",
            mem_exponent.astype(jnp.bfloat16),
            mem_value_heads,
            preferred_element_type=jnp.float32,
        ),
    )

    def forward_step(carried, pieces, first_row):
        return softmax_update(carried, pieces, first_row, query_heads, lengths)

    row_max, row_total, weighted = in_blocks(
        forward_step,
        start_state,
        (
            lax.all_gather(key, "ctx", axis=1, tiled=True),
            lax.all_gather(value, "ctx", axis=1, tiled=True),
        ),
        jnp.int32(0),
        1,
    )
    log_total = row_max + jnp.log(row_total)
    attended_full = (weighted / row_total[..., None]).reshape(seq_count, local_len, features)
    attended = attended_full.astype(jnp.bfloat16).reshape(seq_count * local_len, features)
    branch = matmul(attended, full_out) + to_float(bias_out)
    normed, unit_one, inverse_one = norm_forward(
        to_float(token_rows) + branch, to_float(gain_one), to_float(offset_one)
    )
    normed_low = normed.astype(jnp.bfloat16)
    pre_act = matmul(normed_low, full_up) + to_float(bias_up)
    activated, act_pullback = jax.vjp(smooth_act, pre_act)
    hidden = activated.astype(jnp.bfloat16)
    ffn_out = matmul(hidden, full_down) + to_float(bias_down)
    output_rows, unit_two, inverse_two = norm_forward(
        normed + ffn_out, to_float(gain_two), to_float(offset_two)
    )
    layer_out = output_rows.astype(jnp.bfloat16).reshape(seq_count, local_len, features)
    valid_rows = key_mask.astype(jnp.float32)
    input_squares = jnp.sum(jnp.square(to_float(inputs)), axis=2)
    branch_squares = jnp.sum(jnp.square(branch), axis=1).reshape(seq_count, local_len)
    ffn_squares = jnp.sum(jnp.square(ffn_out), axis=1).reshape(seq_count, local_len)
    squares = jnp.stack(
        [
            jnp.sum(valid_rows * input_squares, axis=1),
            jnp.sum(valid_rows * branch_squares, axis=1),
            jnp.sum(valid_rows * ffn_squares, axis=1),
        ],
        axis=1,
    )
    squares = lax.psum(squares, "ctx")
    stream_rms = jnp.sqrt(squares / (lengths.astype(jnp.float32)[:, None] * features))
    back_query, back_key, back_value, back_out, back_up, back_down, back_gain_one, back_gain_two = (
        lax.all_gather(w_query, "shard", axis=0, tiled=True),
        lax.all_gather(w_key, "shard", axis=0, tiled=True),
        lax.all_gather(w_value, "shard", axis=0, tiled=True),
        lax.all_gather(w_out, "shard", axis=0, tiled=True),
        lax.all_gather(w_up, "shard", axis=0, tiled=True),
        lax.all_gather(w_down, "shard", axis=0, tiled=True),
        lax.all_gather(first_gain, "shard", axis=0, tiled=True),
        lax.all_gather(second_gain, "shard", axis=0, tiled=True),
    )
    cotangent = to_float(out_grad).reshape(seq_count * local_len, features)
    grad_two, grad_gain_two, grad_offset_two = norm_backward(
        cotangent, unit_two, inverse_two, to_float(back_gain_two)
    )
    grad_ffn = grad_two.astype(jnp.bfloat16)
    grad_bias_down = jnp.sum(grad_ffn, axis=0, dtype=jnp.float32)
    grad_full_down = outer_sum(hidden, grad_ffn)
    grad_hidden = back_product(grad_ffn, back_down)
    grad_pre = act_pullback(grad_hidden)[0].astype(jnp.bfloat16)
    grad_bias_up = jnp.sum(grad_pre, axis=0, dtype=jnp.float32)
    grad_full_up = outer_sum(normed_low, grad_pre)
    grad_normed = grad_two + back_product(grad_pre, back_up)
    grad_one, grad_gain_one, grad_offset_one = norm_backward(
        grad_normed, unit_one, inverse_one, to_float(back_gain_one)
    )
    grad_branch = grad_one.astype(jnp.bfloat16)
    grad_bias_out = jnp.sum(grad_branch, axis=0, dtype=jnp.float32)
    grad_full_out = outer_sum(attended, grad_branch)
    grad_att = (
        back_product(grad_branch, back_out)
        .astype(jnp.bfloat16)
        .reshape(seq_count, local_len, features)
    )
    row_delta = jnp.sum(
        (to_float(grad_att) * attended_full).reshape(seq_count, local_len, HEADS, HEAD_DIM), axis=-1
    )
    log_all, delta_all = (
        lax.all_gather(log_total, "ctx", axis=1, tiled=True),
        lax.all_gather(row_delta, "ctx", axis=1, tiled=True),
    )
    grad_heads = split_heads(grad_att)
    mem_probs = jnp.exp(head_scores(query_heads, mem_key_heads) - log_total[..., None])
    mem_dots = jnp.einsum(
        "sqhd,skhd->sqhk", grad_heads, mem_value_heads, preferred_element_type=jnp.float32
    )
    mem_dscores = (mem_probs * (mem_dots - row_delta[..., None])).astype(jnp.bfloat16)
    start_query = jnp.einsum(
        "sqhk,skhd->sqhd", mem_dscores, mem_key_heads, preferred_element_type=jnp.float32
    ) * HEAD_DIM ** (-0.5)
    mem_grad_key = jnp.einsum(
        "sqhk,sqhd->skhd", mem_dscores, query_heads, preferred_element_type=jnp.float32
    ) * HEAD_DIM ** (-0.5)
    mem_grad_value = jnp.einsum(
        "sqhk,sqhd->skhd",
        mem_probs.astype(jnp.bfloat16),
        grad_heads,
        preferred_element_type=jnp.float32,
    )
    key_heads = split_heads(key)
    value_heads = split_heads(value)
    empty_grads = jnp.zeros(key_heads.shape, jnp.float32)

    def query_step(carried, pieces, first_row):
        return query_update(
            carried, pieces, first_row, query_heads, grad_heads, log_total, row_delta, lengths
        )

    def key_step(carried, pieces, first_row):
        return key_update(
            carried, pieces, first_row, key_heads, value_heads, log_all, delta_all, key_mask
        )

    grad_q = in_blocks(
        query_step,
        start_query,
        (
            lax.all_gather(key, "ctx", axis=1, tiled=True),
            lax.all_gather(value, "ctx", axis=1, tiled=True),
        ),
        jnp.int32(0),
        1,
    )
    grad_k, grad_v = in_blocks(
        key_step,
        (empty_grads, empty_grads),
        (
            lax.all_gather(query, "ctx", axis=1, tiled=True),
            lax.all_gather(grad_att, "ctx", axis=1, tiled=True),
        ),
        jnp.int32(0),
        1,
    )
    mem_key_sum, mem_value_sum = lax.psum((mem_grad_key, mem_grad_value), "ctx")
    mem_key_low = mem_key_sum.reshape(seq_count * mem_rows, features).astype(jnp.bfloat16)
    mem_value_low = mem_value_sum.reshape(seq_count * mem_rows, features).astype(jnp.bfloat16)
    first_only = (lax.axis_index("ctx") == 0).astype(jnp.float32)
    grad_q_low = grad_q.reshape(seq_count * local_len, features).astype(jnp.bfloat16)
    grad_k_low = grad_k.reshape(seq_count * local_len, features).astype(jnp.bfloat16)
    grad_v_low = grad_v.reshape(seq_count * local_len, features).astype(jnp.bfloat16)
    grad_full_query = outer_sum(token_rows, grad_q_low)
    grad_full_key = outer_sum(token_rows, grad_k_low) + first_only * outer_sum(
        mem_flat, mem_key_low
    )
    grad_full_value = outer_sum(token_rows, grad_v_low) + first_only * outer_sum(
        mem_flat, mem_value_low
    )
    grad_bias_query = jnp.sum(grad_q_low, axis=0, dtype=jnp.float32)
    grad_bias_value = jnp.sum(grad_v_low, axis=0, dtype=jnp.float32) + first_only * jnp.sum(
        mem_value_low, axis=0, dtype=jnp.float32
    )
    input_grad = (
        grad_one
        + back_product(grad_q_low, back_query)
        + back_product(grad_k_low, back_key)
        + back_product(grad_v_low, back_value)
    ).reshape(seq_count, local_len, features)
    memory_grad = (
        back_product(mem_key_low, back_key) + back_product(mem_value_low, back_value)
    ).reshape(seq_count, mem_rows, features)
    owned_parts = (
        lax.psum_scatter(
            grad_full_query.astype(jnp.bfloat16), "shard", scatter_dimension=0, tiled=True
        ).astype(jnp.float32),
        lax.psum_scatter(
            grad_full_key.astype(jnp.bfloat16), "shard", scatter_dimension=0, tiled=True
        ).astype(jnp.float32),
        lax.psum_scatter(
            grad_full_value.astype(jnp.bfloat16), "shard", scatter_dimension=0, tiled=True
        ).astype(jnp.float32),
        lax.psum_scatter(
            grad_full_out.astype(jnp.bfloat16), "shard", scatter_dimension=0, tiled=True
        ).astype(jnp.float32),
        lax.psum_scatter(
            grad_full_up.astype(jnp.bfloat16), "shard", scatter_dimension=0, tiled=True
        ).astype(jnp.float32),
        lax.psum_scatter(
            grad_full_down.astype(jnp.bfloat16), "shard", scatter_dimension=0, tiled=True
        ).astype(jnp.float32),
        lax.psum_scatter(
            grad_bias_query.astype(jnp.bfloat16), "shard", scatter_dimension=0, tiled=True
        ).astype(jnp.float32),
        lax.psum_scatter(
            grad_bias_value.astype(jnp.bfloat16), "shard", scatter_dimension=0, tiled=True
        ).astype(jnp.float32),
        lax.psum_scatter(
            grad_bias_out.astype(jnp.bfloat16), "shard", scatter_dimension=0, tiled=True
        ).astype(jnp.float32),
        lax.psum_scatter(
            grad_bias_up.astype(jnp.bfloat16), "shard", scatter_dimension=0, tiled=True
        ).astype(jnp.float32),
        lax.psum_scatter(
            grad_bias_down.astype(jnp.bfloat16), "shard", scatter_dimension=0, tiled=True
        ).astype(jnp.float32),
        lax.psum_scatter(
            grad_gain_one.astype(jnp.bfloat16), "shard", scatter_dimension=0, tiled=True
        ).astype(jnp.float32),
        lax.psum_scatter(
            grad_offset_one.astype(jnp.bfloat16), "shard", scatter_dimension=0, tiled=True
        ).astype(jnp.float32),
        lax.psum_scatter(
            grad_gain_two.astype(jnp.bfloat16), "shard", scatter_dimension=0, tiled=True
        ).astype(jnp.float32),
        lax.psum_scatter(
            grad_offset_two.astype(jnp.bfloat16), "shard", scatter_dimension=0, tiled=True
        ).astype(jnp.float32),
    )
    (
        part_query,
        part_key,
        part_value,
        part_out,
        part_up,
        part_down,
        part_bias_query,
        part_bias_value,
        part_bias_out,
        part_bias_up,
        part_bias_down,
        part_gain_one,
        part_offset_one,
        part_gain_two,
        part_offset_two,
    ) = owned_parts
    summed_grads = lax.psum(
        (
            part_query,
            part_key,
            part_value,
            part_out,
            part_up,
            part_down,
            part_bias_query,
            part_bias_value,
            part_bias_out,
            part_bias_up,
            part_bias_down,
            part_gain_one,
            part_offset_one,
            part_gain_two,
            part_offset_two,
        ),
        "ctx",
    )
    (
        sum_query,
        sum_key,
        sum_value,
        sum_out,
        sum_up,
        sum_down,
        sum_bias_query,
        sum_bias_value,
        sum_bias_out,
        sum_bias_up,
        sum_bias_down,
        sum_gain_one,
        sum_offset_one,
        sum_gain_two,
        sum_offset_two,
    ) = summed_grads
    return (
        layer_out,
        input_grad,
        memory_grad,
        sum_query,
        sum_key,
        sum_value,
        sum_out,
        sum_up,
        sum_down,
        sum_bias_query,
        sum_bias_value,
        sum_bias_out,
        sum_bias_up,
        sum_bias_down,
        sum_gain_one,
        sum_offset_one,
        sum_gain_two,
        sum_offset_two,
        stream_rms,
    )


def solution(mesh):
    in_specs = (
        P("shard", "ctx", None),
        P("shard", None, None),
        P("shard"),
        P("shard", None),
        P("shard", None),
        P("shard", None),
        P("shard", None),
        P("shard", None),
        P("shard", None),
        P("shard"),
        P("shard"),
        P("shard"),
        P("shard"),
        P("shard"),
        P("shard"),
        P("shard"),
        P("shard"),
        P("shard"),
        P("shard", "ctx", None),
    )
    out_specs = (
        P("shard", "ctx", None),
        P("shard", "ctx", None),
        P("shard", None, None),
        P("shard", None),
        P("shard", None),
        P("shard", None),
        P("shard", None),
        P("shard", None),
        P("shard", None),
        P("shard"),
        P("shard"),
        P("shard"),
        P("shard"),
        P("shard"),
        P("shard"),
        P("shard"),
        P("shard"),
        P("shard"),
        P("shard", None),
    )
    return jax.shard_map(local, mesh=mesh, in_specs=in_specs, out_specs=out_specs, check_vma=False)
```

profile of v0, /device:TPU:0, one launch (start us, length us, event | category | flops | bytes accessed | tf_op | source)
XLA Modules:
  0.0 575.2 jit_solution(16978654707949027786)
XLA Ops:
  7.2 9.0 %all_gather.75 = bf16[512,512]{1,0:T(8,128)(2,1)S(1)} all-gather(bf16[128,512]{1,0:T(8,128)(2,1)} %param.23), channel_id=1, replica_groups=mesh['shard'=4,'ctx'=8] {'shard'}, dimensions={0}, use_global_device_ids=true | all-gather | bytes 655360 | tf_op jit(solution)/shard_map/all_gather | solution.py:180
  16.2 2.0 convolution_convert_fusion.5
  18.3 5.2 all-gather
  23.5 7.4 %all_gather.73 = bf16[512,512]{1,0:T(8,128)(2,1)S(1)} all-gather(bf16[128,512]{1,0:T(8,128)(2,1)} %param.24), channel_id=1, replica_groups=mesh['shard'=4,'ctx'=8] {'shard'}, dimensions={0}, use_global_device_ids=true | all-gather | bytes 655360 | tf_op jit(solution)/shard_map/all_gather | solution.py:181
  30.9 1.0 fusion.54
  33.4 5.0 all-gather.1
  38.4 7.2 %all_gather.76 = bf16[512,512]{1,0:T(8,128)(2,1)S(1)} all-gather(bf16[128,512]{1,0:T(8,128)(2,1)S(1)} %copy-done.31), channel_id=1, replica_groups=mesh['shard'=4,'ctx'=8] {'shard'}, dimensions={0}, use_global_device_ids=true | all-gather | bytes 655360 | tf_op jit(solution)/shard_map/all_gather | solution.py:179
  46.4 1.0 fusion.53
  47.6 1.3 reshape.314
  49.3 5.0 all-gather.4
  55.0 5.0 all-gather.3
  60.0 5.0 all-gather.2
  65.6 7.7 %all_gather.80 = bf16[512,512]{1,0:T(8,128)(2,1)} all-gather(bf16[128,512]{1,0:T(8,128)(2,1)S(1)} %copy-done.32), channel_id=1, replica_groups=mesh['shard'=4,'ctx'=8] {'shard'}, dimensions={0}, use_global_device_ids=true | all-gather | bytes 655360 | tf_op jit(solution)/shard_map/all_gather | solution.py:182
  74.6 5.0 all-gather.6
  80.2 5.1 all-gather.5
  85.4 5.0 all-gather.7
  90.4 5.0 all-gather.8
  98.3 3.0 copy.136
  101.3 3.4 bitcast_reduce_fusion
  104.8 3.2 copy-done
  108.0 1.8 fusion.7
  109.9 9.2 %all-gather.18.cloned.1.call-done = bf16[2,1024,512]{2,1,0:T(8,128)(2,1)} async-done(((bf16[2,128,512]{2,1,0:T(8,128)(2,1)}), bf16[2,1024,512]{2,1,0:T(8,128)(2,1)}) %all-gather.18.cloned.1.call-update) | async-done | bytes 2097168 | tf_op jit(solution)/shard_map/all_gather | solution.py:260
  119.1 4.1 copy.138
  123.2 7.0 %fusion.44 = f32[2,128,8,64]{1,3,2,0:T(8,128)S(1)} fusion(bf16[2,1024,8,64]{1,3,2,0:T(8,128)(2,1)} %bitcast.269, f32[2,8,1024,128]{3,2,1,0:T(8,128)} %copy-done, f32[2,128,8]{1,2,0:T(8,128)S(1)} %max.16, pred[2,1024]{1,0:T(4,128)(4,1)S(1)} %iota_compare_fusion), kind=kOutput, calls=%fused_computation.59 | convolution fusion | flops 276824064 | bytes 11020288 | tf_op jit(solution)/shard_map/sqhk,skhd->sqhd/dot_general | solution.py:104
  130.3 1.1 fusion.138
  132.6 9.2 %all-gather.20.cloned.1.call-done = bf16[512,2048]{1,0:T(8,128)(2,1)} async-done(((bf16[128,2048]{1,0:T(8,128)(2,1)}), bf16[512,2048]{1,0:T(8,128)(2,1)}) %all-gather.20.cloned.1.call-update) | async-done | bytes 2097168 | tf_op jit(solution)/shard_map/all_gather | solution.py:183
  141.8 3.7 convolution_add_fusion
  145.4 20.4 %all-gather.22.cloned.1.call-done = bf16[2048,512]{1,0:T(8,128)(2,1)} async-done(((bf16[512,512]{1,0:T(8,128)(2,1)}), bf16[2048,512]{1,0:T(8,128)(2,1)}) %all-gather.22.cloned.1.call-update) | async-done | bytes 2097168 | tf_op jit(solution)/shard_map/all_gather | solution.py:184
  165.8 3.4 fusion.134
  169.4 1.5 fusion.81
  171.8 2.5 fusion.140
  174.3 1.5 multiply_reduce_fusion.3
  176.9 1.1 reshape.315
  178.0 1.3 copy.143
  179.3 1.1 multiply_reduce_fusion.4
  180.4 1.7 fusion.69
  182.2 9.6 %fusion.14 = f32[2,8,64,128]{3,2,1,0:T(8,128)} fusion(bf16[2,1024,8,64]{1,3,2,0:T(8,128)(2,1)} %bitcast.256, f32[2,8,1024,128]{3,2,1,0:T(8,128)} %copy-done, f32[2,128,8]{1,2,0:T(8,128)S(1)} %multiply_reduce_fusion.4, f32[2,128,8]{1,2,0:T(8,128)S(1)} %get-tuple-element.136, pred[2,1024]{1,0:T(4,128)(4,1)S(1)} %iota_compare_fusion, ...), kind=kOutput, calls=%fused_computation.19 | convolution fusion | flops 549453824 | bytes 13387776 | tf_op jit(solution)/shard_map/sqhk,skhd->sqhd/dot_general | solution.py:125
  191.8 1.5 fusion.139
  194.3 1.1 fusion.39
  195.4 2.0 copy.176
  197.5 1.1 convolution_convert_fusion.2
  199.5 3.5 convolution_convert_fusion.1
  203.0 1.1 reshape.297
  204.1 1.1 reshape.298
  208.1 4.0 convolution_convert_fusion
  212.5 41.7 %all-reduce.14 = (bf16[2,20,8,64]{3,2,1,0:T(8,128)(2,1)S(1)}, bf16[2,20,8,64]{3,1,2,0:T(8,128)(2,1)S(1)}) all-reduce(f32[2,20,8,64]{3,2,1,0:T(8,128)S(1)} %fusion.105, f32[2,20,8,64]{3,1,2,0:T(8,128)S(1)} %convolution_bitcast_fusion.1), channel_id=1, replica_groups=mesh['shard'=4,'ctx'=8] {'ctx'}, use_global_device_ids=true, to_apply=%region_13.14 | all-reduce | flops 40960 | bytes 245760 | tf_op jit(solution)/shard_map/psum | solution.py:387
  255.9 4.0 copy.149
  259.9 32.3 %all_gather.93 = f32[2,1024,8]{1,2,0:T(8,128)} all-gather(f32[2,128,8]{1,2,0:T(8,128)S(1)} %multiply_reduce_fusion.4), channel_id=1, replica_groups=mesh['shard'=4,'ctx'=8] {'ctx'}, dimensions={1}, use_global_device_ids=true | all-gather | bytes 73728 | tf_op jit(solution)/shard_map/all_gather | solution.py:333
  292.2 32.4 %all_gather.91 = f32[2,1024,8]{1,2,0:T(8,128)} all-gather(f32[2,128,8]{1,2,0:T(8,128)S(1)} %get-tuple-element.136), channel_id=1, replica_groups=mesh['shard'=4,'ctx'=8] {'ctx'}, dimensions={1}, use_global_device_ids=true | all-gather | bytes 73728 | tf_op jit(solution)/shard_map/all_gather | solution.py:332
  325.4 1.1 convolution_add_fusion.6
  326.6 4.5 fusion.73
  331.0 1.7 copy.177
  332.7 4.4 copy.153
  337.2 8.6 %fusion.63 = bf16[2,128,8,64]{1,3,2,0:T(8,128)(2,1)} fusion(bf16[2,1024,8,64]{1,3,2,0:T(8,128)(2,1)S(1)} %bitcast.258, f32[2,8,128,1024]{3,2,1,0:T(8,128)} %fusion.73, f32[2,1024,8]{1,2,0:T(8,128)} %all_gather.93, f32[2,1024,8]{1,2,0:T(8,128)} %all_gather.91, pred[2,128]{1,0:T(4,128)(4,1)S(1)} %copy-done.60, bf16[2,1024,8,64]{1,3,2,0:T(8,128)(2,1)} %bitcast.271, ...), kind=kOutput, calls=%fused_computation.76 | convolution fusion | flops 549715968 | bytes 13238528 | tf_op jit(solution)/shard_map/sqhk,sqhd->skhd/dot_general | solution.py:151
  345.7 1.2 copy.156
  347.0 6.1 %convert_reduce_fusion = (f32[8,64]{1,0:T(8,128)S(1)}, bf16[2,128,8,64]{1,3,2,0:T(8,128)(2,1)S(1)}) fusion(bf16[2,1024,8,64]{1,3,2,0:T(8,128)(2,1)} %bitcast.272, f32[2,8,128,1024]{3,2,1,0:T(8,128)} %fusion.73, f32[2,1024,8]{1,2,0:T(8,128)} %all_gather.91, pred[2,128]{1,0:T(4,128)(4,1)S(1)} %copy-done.60), kind=kOutput, calls=%fused_computation.105 | convolution fusion | flops 277216768 | bytes 10815744 | tf_op jit(solution)/shard_map/sqhk,sqhd->skhd/dot_general | solution.py:141
  356.9 10.1 %all-reduce.11 = (bf16[512]{0:T(512)(128)(2,1)S(1)}, bf16[512]{0:T(512)(128)(2,1)S(1)}, bf16[512]{0:T(512)(128)(2,1)S(1)}, bf16[2048]{0:T(1024)(128)(2,1)S(1)}, ...) all-reduce(bf16[512]{0:T(512)(128)(2,1)S(1)} %reduce_sum.272, ...), channel_id=8, replica_groups=mesh['shard'=4,'ctx'=8] {'shard'}, use_global_device_ids=true, to_apply=%region_28.29.clone | all-reduce | flops 6144 | bytes 24576
  368.1 1.1 convolution_add_fusion.4
  369.2 14.0 %reduce-scatter.17.cloned.1.call-done = bf16[512,512]{1,0:T(8,128)(2,1)} async-done(((bf16[2048,512]{1,0:T(8,128)(2,1)}), bf16[512,512]{1,0:T(8,128)(2,1)}) %reduce-scatter.17.cloned.1.call-update) | async-done | bytes 524304 | tf_op jit(solution)/shard_map/reduce_scatter | solution.py:430
  383.2 24.7 %reduce-scatter.21.cloned.1.call-done = bf16[128,512]{1,0:T(8,128)(2,1)} async-done(((bf16[512,512]{1,0:T(8,128)(2,1)}), bf16[128,512]{1,0:T(8,128)(2,1)}) %reduce-scatter.21.cloned.1.call-update) | async-done | bytes 131088
  407.9 1.0 copy.179
  408.9 23.8 %reduce-scatter.23.cloned.1.call-done = bf16[128,512]{1,0:T(8,128)(2,1)} async-done(((bf16[512,512]{1,0:T(8,128)(2,1)}), bf16[128,512]{1,0:T(8,128)(2,1)}) %reduce-scatter.23.cloned.1.call-update) | async-done | bytes 131088
  432.7 1.0 copy.181
  433.7 131.0 %all-reduce.15 = (f32[128,512]{0,1:T(8,128)S(1)}, f32[128,512]{0,1:T(8,128)S(1)}, f32[128,512]{0,1:T(8,128)S(1)}, f32[128,512]{1,0:T(8,128)}, f32[128,2048]{1,0:...) all-reduce(bf16[128,512]{0,1:T(8,128)(2,1)S(1)} %copy-done.28, ...), channel_id=1, replica_groups=mesh['shard'=4,'ctx'=8] {'ctx'}, use_global_device_ids=true, to_apply=%region_16.17 | all-reduce | flops 787974 | bytes 4730928 | tf_op jit(solution)/shard_map/psum | solution.py:478
  (236 shorter events, 26.2 us)
Async XLA Ops:
  7.2 23.7 %copy-start.1 = (bf16[2,128,512]{2,1,0:T(8,128)(2,1)S(1)}, bf16[2,128,512]{2,1,0:T(8,128)(2,1)}, u32[]{:S(2)}) copy-start(bf16[2,128,512]{2,1,0:T(8,128)(2,1)} %param.19) | copy-start | bytes 786436
  7.2 91.1 %all-gather.16.cloned.1.call-start = ((), (), s32[]{:S(2)}) async-start(), calls=%async_computation.6 | async-start | bytes 2359296 | tf_op jit(solution)/shard_map/all_gather | solution.py:259
  16.2 17.1 %copy-start.52 = (bf16[128]{0:T(256)(128)(2,1)S(1)}, bf16[128]{0:T(256)(128)(2,1)}, u32[]{:S(2)}) copy-start(bf16[128]{0:T(256)(128)(2,1)} %param.28) | copy-start | bytes 772
  16.2 22.2 %copy-start.31 = (bf16[128,512]{1,0:T(8,128)(2,1)S(1)}, bf16[128,512]{1,0:T(8,128)(2,1)}, u32[]{:S(2)}) copy-start(bf16[128,512]{1,0:T(8,128)(2,1)} %param.22) | copy-start | bytes 393220
  18.2 100.9 %all-gather.18.cloned.1.call-start = ((), (), s32[]{:S(2)}) async-start(), calls=%async_computation.7 | async-start | bytes 2359296 | tf_op jit(solution)/shard_map/all_gather | solution.py:260
  31.9 17.0 %copy-start.34 = (bf16[2,20,512]{2,0,1:T(2,128)(2,1)S(1)}, bf16[2,20,512]{2,0,1:T(2,128)(2,1)}, u32[]{:S(2)}) copy-start(bf16[2,20,512]{2,0,1:T(2,128)(2,1)} %param.20) | copy-start | bytes 122884
  31.9 109.8 %all-gather.20.cloned.1.call-start = ((), (), s32[]{:S(2)}) async-start(), calls=%async_computation.8 | async-start | bytes 2621440 | tf_op jit(solution)/shard_map/all_gather | solution.py:183
  32.7 133.1 %all-gather.22.cloned.1.call-start = ((), (), s32[]{:S(2)}) async-start(), calls=%async_computation.9 | async-start | bytes 2621440 | tf_op jit(solution)/shard_map/all_gather | solution.py:184
  33.3 16.1 %copy-start.53 = (bf16[128]{0:T(256)(128)(2,1)S(1)}, bf16[128]{0:T(256)(128)(2,1)}, u32[]{:S(2)}) copy-start(bf16[128]{0:T(256)(128)(2,1)} %param.34) | copy-start | bytes 772
  33.3 21.7 %copy-start.54 = (bf16[128]{0:T(256)(128)(2,1)S(1)}, bf16[128]{0:T(256)(128)(2,1)}, u32[]{:S(2)}) copy-start(bf16[128]{0:T(256)(128)(2,1)} %param.33) | copy-start | bytes 772
  33.3 26.7 %copy-start.55 = (bf16[128]{0:T(256)(128)(2,1)S(1)}, bf16[128]{0:T(256)(128)(2,1)}, u32[]{:S(2)}) copy-start(bf16[128]{0:T(256)(128)(2,1)} %param.30) | copy-start | bytes 772
  33.3 32.3 %copy-start.32 = (bf16[128,512]{1,0:T(8,128)(2,1)S(1)}, bf16[128,512]{1,0:T(8,128)(2,1)}, u32[]{:S(2)}) copy-start(bf16[128,512]{1,0:T(8,128)(2,1)} %param.25) | copy-start | bytes 393220
  33.3 222.5 %all-gather.24.cloned.1.call-start = ((), (), s32[]{:S(2)}) async-start(), calls=%async_computation.10 | async-start | bytes 2359296 | tf_op jit(solution)/shard_map/all_gather | solution.py:381
  47.4 26.3 %copy-start.45 = (s32[2]{0:T(128)S(1)}, s32[2]{0:T(128)}, u32[]{:S(2)}) copy-start(s32[2]{0:T(128)} %param.21) | copy-start | bytes 28
  47.4 27.1 %copy-start.56 = (bf16[128]{0:T(256)(128)(2,1)S(1)}, bf16[128]{0:T(256)(128)(2,1)}, u32[]{:S(2)}) copy-start(bf16[128]{0:T(256)(128)(2,1)} %param.32) | copy-start | bytes 772
  47.4 32.7 %copy-start.49 = (bf16[512]{0:T(512)(128)(2,1)S(1)}, bf16[512]{0:T(512)(128)(2,1)}, u32[]{:S(2)}) copy-start(bf16[512]{0:T(512)(128)(2,1)} %param.31) | copy-start | bytes 3076
  47.4 37.9 %copy-start.57 = (bf16[128]{0:T(256)(128)(2,1)S(1)}, bf16[128]{0:T(256)(128)(2,1)}, u32[]{:S(2)}) copy-start(bf16[128]{0:T(256)(128)(2,1)} %param.35) | copy-start | bytes 772
  47.5 43.0 %copy-start.58 = (bf16[128]{0:T(256)(128)(2,1)S(1)}, bf16[128]{0:T(256)(128)(2,1)}, u32[]{:S(2)}) copy-start(bf16[128]{0:T(256)(128)(2,1)} %param.36) | copy-start | bytes 772
  47.5 48.6 %copy-start.7 = (bf16[2,128,512]{2,1,0:T(8,128)(2,1)S(1)}, bf16[2,128,512]{2,1,0:T(8,128)(2,1)}, u32[]{:S(2)}) copy-start(bf16[2,128,512]{2,1,0:T(8,128)(2,1)} %param.37) | copy-start | bytes 786436
  47.5 283.5 %reduce-scatter.19.cloned.1.call-start = ((), (), s32[]{:S(2)}) async-start(), calls=%async_computation.15 | async-start | bytes 655360
  73.6 24.7 %copy-start.9 = (bf16[2,128,8,64]{1,3,2,0:T(8,128)(2,1)}, bf16[2,128,8,64]{1,3,2,0:T(8,128)(2,1)S(1)}, u32[]{:S(2)}) copy-start(bf16[2,128,8,64]{1,3,2,0:T(8,128)(2,1)S(1)} %copy.134) | copy-start | bytes 786436
  90.4 5.8 %copy-start.36 = (f32[4,1,128]{2,1,0:T(1,128)}, f32[4,1,128]{2,1,0:T(1,128)S(1)}, u32[]{:S(2)}) copy-start(f32[4,1,128]{2,1,0:T(1,128)S(1)} %convert_element_type.355) | copy-start | bytes 6148
  101.3 3.5 copy-start.2
  104.8 3.2 copy-start
  123.2 7.0 %copy-start.38 = (f32[2,128,8]{1,2,0:T(8,128)S(1)}, f32[2,128,8]{1,2,0:T(8,128)}, u32[]{:S(2)}) copy-start(f32[2,128,8]{1,2,0:T(8,128)} %fusion.102) | copy-start | bytes 24580
  123.2 7.1 %copy-start.12 = (f32[2,128,8,20]{1,3,2,0:T(8,128)S(1)}, f32[2,128,8,20]{1,3,2,0:T(8,128)}, u32[]{:S(2)}) copy-start(f32[2,128,8,20]{1,3,2,0:T(8,128)} %copy-done.11) | copy-start | bytes 491524
  123.2 7.1 %copy-start.30 = (bf16[2,20,8,64]{3,2,1,0:T(8,128)(2,1)S(1)}, bf16[2,20,8,64]{3,2,1,0:T(8,128)(2,1)}, u32[]{:S(2)}) copy-start(bf16[2,20,8,64]{3,2,1,0:T(8,128)(2,1)} %reshape_reshape.18) | copy-start | bytes 122884
  130.3 11.5 %copy-start.35 = (f32[4,1,128]{2,1,0:T(1,128)S(1)}, f32[4,1,128]{2,1,0:T(1,128)}, u32[]{:S(2)}) copy-start(f32[4,1,128]{2,1,0:T(1,128)} %convert_element_type.352) | copy-start | bytes 6148
  141.8 24.0 %copy-start.47 = (f32[4,1,128]{2,1,0:T(1,128)S(1)}, f32[4,1,128]{2,1,0:T(1,128)}, u32[]{:S(2)}) copy-start(f32[4,1,128]{2,1,0:T(1,128)} %convert_element_type.354) | copy-start | bytes 6148
  165.8 3.6 copy-start.8
  165.8 3.6 copy-start.37
  165.8 3.6 copy-start.39
  165.8 5.2 copy-start.44
  165.8 6.0 %copy-start.61 = (bf16[2048,512]{1,0:T(8,128)(2,1)S(1)}, bf16[2048,512]{1,0:T(8,128)(2,1)}, u32[]{:S(2)}) copy-start(bf16[2048,512]{1,0:T(8,128)(2,1)} %all-gather.22.cloned.1.call-done) | copy-start | bytes 6291460
  169.2 2.6 copy-start.19
  171.8 2.5 copy-start.29
  171.8 2.5 copy-start.20
  174.2 2.3 copy-start.22
  176.9 14.9 %copy-start.13 = (bf16[256,512]{1,0:T(8,128)(2,1)}, bf16[256,512]{1,0:T(8,128)(2,1)S(1)}, u32[]{:S(2)}) copy-start(bf16[256,512]{1,0:T(8,128)(2,1)S(1)} %convolution_convert_fusion.4) | copy-start | bytes 786436
  193.3 4.2 copy-start.25
  197.5 135.3 %reduce-scatter.13.cloned.1.call-start = ((), (), s32[]{:S(2)}) async-start(), calls=%async_computation.12 | async-start | bytes 655360 | tf_op jit(solution)/shard_map/reduce_scatter | solution.py:424
  198.7 134.1 %all-gather.26.cloned.1.call-start = ((), (), s32[]{:S(2)}) async-start(), calls=%async_computation.11 | async-start | bytes 2359296 | tf_op jit(solution)/shard_map/all_gather | solution.py:382
  199.4 3.6 copy-start.14
  199.4 169.8 %reduce-scatter.15.cloned.1.call-start = ((), (), s32[]{:S(2)}) async-start(), calls=%async_computation.13 | async-start | bytes 2621440 | tf_op jit(solution)/shard_map/reduce_scatter | solution.py:427
  202.9 2.3 copy-start.62
  202.9 4.3 copy-start.46
  202.9 4.9 copy-start.10
  202.9 4.9 copy-start.27
  203.0 180.2 %reduce-scatter.17.cloned.1.call-start = ((), (), s32[]{:S(2)}) async-start(), calls=%async_computation.14 | async-start | bytes 2621440 | tf_op jit(solution)/shard_map/reduce_scatter | solution.py:430
  212.2 195.7 %reduce-scatter.21.cloned.1.call-start = ((), (), s32[]{:S(2)}) async-start(), calls=%async_computation.16 | async-start | bytes 655360
  255.8 69.6 %copy-start.6 = (bf16[512,512]{1,0:T(8,128)(2,1)S(1)}, bf16[512,512]{1,0:T(8,128)(2,1)}, u32[]{:S(2)}) copy-start(bf16[512,512]{1,0:T(8,128)(2,1)} %copy-done.5) | copy-start | bytes 1572868
  255.8 69.6 %copy-start.17 = (bf16[2,128,8,64]{1,0,3,2:T(2,128)(2,1)S(1)}, bf16[2,128,8,64]{1,0,3,2:T(2,128)(2,1)}, u32[]{:S(2)}) copy-start(bf16[2,128,8,64]{1,0,3,2:T(2,128)(2,1)} %copy-done.16) | copy-start | bytes 786436
  255.8 70.7 %copy-start.23 = (bf16[2,128,8,64]{3,2,1,0:T(8,128)(2,1)S(1)}, bf16[2,128,8,64]{3,2,1,0:T(8,128)(2,1)}, u32[]{:S(2)}) copy-start(bf16[2,128,8,64]{3,2,1,0:T(8,128)(2,1)} %reshape.297) | copy-start | bytes 786436
  259.9 66.7 %copy-start.3 = (bf16[2,1024,512]{1,2,0:T(8,128)(2,1)S(1)}, bf16[2,1024,512]{1,2,0:T(8,128)(2,1)}, u32[]{:S(2)}) copy-start(bf16[2,1024,512]{1,2,0:T(8,128)(2,1)} %copy.149) | copy-start | bytes 6291460
  332.7 4.4 copy-start.4
  332.7 4.4 copy-start.60
  355.0 77.7 %reduce-scatter.23.cloned.1.call-start = ((), (), s32[]{:S(2)}) async-start(), calls=%async_computation.17 | async-start | bytes 655360
  355.0 1.8 copy-start.40
  355.1 1.8 copy-start.41
  355.1 1.8 copy-start.42
  355.1 12.6 %copy-start.18 = (f32[256,512]{1,0:T(8,128)S(1)}, f32[256,512]{1,0:T(8,128)}, u32[]{:S(2)}) copy-start(f32[256,512]{1,0:T(8,128)} %convolution_add_fusion.6) | copy-start | bytes 1572868
  367.7 66.0 %copy-start.28 = (bf16[128,512]{0,1:T(8,128)(2,1)S(1)}, bf16[128,512]{0,1:T(8,128)(2,1)}, u32[]{:S(2)}) copy-start(bf16[128,512]{0,1:T(8,128)(2,1)} %copy.177) | copy-start | bytes 393220
  367.7 66.0 %copy-start.33 = (bf16[128,512]{1,0:T(8,128)(2,1)S(1)}, bf16[128,512]{1,0:T(8,128)(2,1)}, u32[]{:S(2)}) copy-start(bf16[128,512]{1,0:T(8,128)(2,1)} %reduce-scatter.13.cloned.1.call-done) | copy-start | bytes 393220
  369.2 198.0 %copy-start.59 = (f32[2]{0:T(128)S(1)}, f32[2]{0:T(128)}, u32[]{:S(2)}) copy-start(f32[2]{0:T(128)} %convert_multiply_fusion.1) | copy-start | bytes 28
  (11 other events, 13.8 us)
Sparse Core Ops, SparseCore 0:
  18.4 50.1 all-gather.15
  71.3 47.7 all-gather.17
  120.7 21.0 all-gather.19
  143.2 22.5 all-gather.21
  168.4 49.2 all-gather.23
  220.0 20.1 reduce-scatter.18
  242.8 21.6 reduce-scatter.12
  266.7 49.3 all-gather.25
  318.6 30.4 reduce-scatter.14
  351.7 31.4 reduce-scatter.16
  386.3 21.6 reduce-scatter.20
  411.0 21.6 reduce-scatter.22
where the time goes:
time: 581 us; the launch traced here: 575 us
  blocking collectives  324 us (56%)
  waiting for transfers between devices  103 us (18%)
  matrix products  74.5 us (13%)
  local copies, waits for them, and re-layouts  43.1 us (7%)
  between operations  16.8 us (3%)
  other arithmetic  12.6 us (2%)
    psum x1, blocking collectives, local(): lax.psum((part_query, part_key, part_value, part_out, part_up, part_down,...  131 us
    unnamed x15, waiting for transfers between devices  50.5 us
    psum x1, blocking collectives, local(): mem_key_sum, mem_value_sum = lax.psum((mem_grad_key, mem_grad_value), 'ctx')  41.7 us
    all_gather x1, blocking collectives, local(): lax.all_gather(log_total, 'ctx', axis=1, tiled=True)  32.4 us
    all_gather x1, blocking collectives, local(): lax.all_gather(row_delta, 'ctx', axis=1, tiled=True)  32.3 us
    all_gather x1, waiting for transfers between devices, local(): lax.all_gather(w_down, 'shard', axis=0, tiled=True)  20.4 us
    unnamed x140, local copies, waits for them, and re-layouts  18.1 us
    reduce_scatter x1, waiting for transfers between devices, local(): lax.psum_scatter(grad_full_down.astype(jnp.bfloat16), 'shard', scatter_di...  14 us
  transfers between devices with their start and end apart: 12, of which 6 were waited for; matrix products, arithmetic and copies ran while one was open for 21% of the time, Pallas kernels for 0%

commit v1 on v0

--- a/solution.py
+++ b/solution.py
@@ -3,10 +3,14 @@
 import jax
 import jax.numpy as jnp
 from jax import lax
+from jax.experimental import pallas as pl
+from jax.experimental.pallas import tpu as pltpu
 from jax.sharding import PartitionSpec as P
 
 HEADS = 8
 HEAD_DIM = 64
+MEM_ROWS = 20
+GELU_SCALE = math.sqrt(2 / math.pi)
 
 
 eps = 1e-05
@@ -535,6 +539,794 @@
     )
 
 
+MESH_ID = pl.DeviceIdType.MESH
+LANES = 128
+MEM_PAD = 32
+ROW_KINDS = 16
+SLOTS = 104
+
+
+def flipped(index, offset, bits):
+    total = 0
+    for bit in range(bits):
+        digit = lax.rem(lax.div(index, 2**bit), 2)
+        if offset >> bit & 1:
+            digit = 1 - digit
+        total = total + digit * 2**bit
+    return total
+
+
+class Copies:
+    def __init__(self, send_sems, recv_sems):
+        self.send_sems, self.recv_sems = send_sems, recv_sems
+        self.started = []
+
+    def send(self, src, dst, device):
+        slot = len(self.started)
+        copy = pltpu.make_async_remote_copy(
+            src_ref=src,
+            dst_ref=dst,
+            send_sem=self.send_sems.at[slot],
+            recv_sem=self.recv_sems.at[slot],
+            device_id=device,
+            device_id_type=MESH_ID,
+        )
+        copy.start()
+        self.started.append(copy)
+        return copy
+
+    def local(self, src, dst):
+        slot = len(self.started)
+        copy = pltpu.make_async_copy(src, dst, self.send_sems.at[slot])
+        copy.start()
+        self.started.append(None)
+        return copy
+
+    def finish(self):
+        for copy in self.started:
+            if copy is not None:
+                copy.wait_send()
+
+
+def layer_kernel(
+    x_ref,
+    g_ref,
+    mem_ref,
+    len_ref,
+    vec_ref,
+    wq_ref,
+    wk_ref,
+    wv_ref,
+    wo_ref,
+    wu_ref,
+    wd_ref,
+    o_layer,
+    o_input,
+    o_mem,
+    o_fin,
+    o_qkv,
+    o_vec,
+    o_rms,
+    tokens,
+    tokens_t,
+    w_heads,
+    w_out,
+    w_up,
+    w_down,
+    vecs,
+    q_scaled,
+    q_aug,
+    k_aug,
+    v_mask,
+    k_turned,
+    v_turned,
+    probs,
+    d_scores,
+    mixed_t,
+    mixed,
+    att,
+    hidden,
+    act_slope,
+    d_pre,
+    d_att,
+    d_mixed,
+    partial,
+    got_core,
+    got_x,
+    got_y,
+    got_z,
+    got_far,
+    final,
+    head_part,
+    head_core,
+    head_x,
+    head_far,
+    head_all,
+    vec_part,
+    dx_part,
+    dx_got,
+    dx_far_sum,
+    dx_far,
+    mem_part,
+    mem_far,
+    squares,
+    send_sems,
+    recv_sems,
+):
+    bf16, f32 = jnp.bfloat16, jnp.float32
+    shard, ctx = lax.axis_index("shard"), lax.axis_index("ctx")
+    span, width = x_ref.shape[1], x_ref.shape[2]
+    spans = 8
+    length_all = span * spans
+    keys = length_all + MEM_PAD
+    x_half, core = lax.div(shard, 2), lax.rem(shard, 2)
+    upper, pair = lax.div(ctx, 4), lax.rem(ctx, 4)
+    y_side = lax.rem(ctx, 2)
+    z_side = lax.rem(lax.div(ctx, 2) + upper, 2)
+
+    def shard_peer(offset):
+        return {"shard": flipped(shard, offset, 2), "ctx": ctx}
+
+    def ctx_peer(offset):
+        return {"shard": shard, "ctx": flipped(ctx, offset, 3)}
+
+    def span_rows(index):
+        return pl.ds(pl.multiple_of(index * span, span), span)
+
+    def pair_lanes(index, size=LANES):
+        return pl.ds(pl.multiple_of(index * LANES, LANES), size)
+
+    copies = Copies(send_sems, recv_sems)
+
+    barrier = pltpu.get_barrier_semaphore()
+    for offset in (1, 2, 3):
+        pl.semaphore_signal(barrier, inc=1, device_id=shard_peer(offset), device_id_type=MESH_ID)
+    for offset in range(1, 8):
+        pl.semaphore_signal(barrier, inc=1, device_id=ctx_peer(offset), device_id_type=MESH_ID)
+    pl.semaphore_wait(barrier, 10)
+
+    far_tokens = copies.send(x_ref.at[1 - upper], tokens.at[span_rows(ctx)], ctx_peer(6))
+    head_copies = []
+    my_rows = pl.ds(pl.multiple_of(shard * LANES, LANES), LANES)
+    for offset in (2, 3, 1):
+        for part, ref in enumerate((wq_ref, wk_ref, wv_ref)):
+            head_copies.append(
+                copies.send(
+                    ref.at[:, pair_lanes(pair)],
+                    w_heads.at[my_rows, pl.ds(part * LANES, LANES)],
+                    shard_peer(offset),
+                )
+            )
+        head_copies.append(copies.send(vec_ref, vecs.at[shard], shard_peer(offset)))
+    near_tokens = [
+        copies.send(x_ref.at[upper], tokens.at[span_rows(ctx)], ctx_peer(offset))
+        for offset in (3, 2, 1)
+    ]
+    local_copies = [
+        copies.local(ref.at[:, pair_lanes(pair)], w_heads.at[my_rows, pl.ds(part * LANES, LANES)])
+        for part, ref in enumerate((wq_ref, wk_ref, wv_ref))
+    ]
+    local_copies.append(copies.local(vec_ref, vecs.at[shard]))
+    local_copies.append(copies.local(x_ref.at[upper], tokens.at[span_rows(ctx)]))
+
+    def rows_of(ref, index):
+        rows = ref.shape[0] // 4
+        return ref.at[pl.ds(pl.multiple_of(index * rows, LANES), rows)]
+
+    full_weights = ((wo_ref, w_out), (wu_ref, w_up), (wd_ref, w_down))
+    from_x = [
+        copies.send(ref, rows_of(full, shard), shard_peer(2)) for ref, full in full_weights
+    ]
+    from_core = [
+        copies.send(ref, rows_of(full, shard), shard_peer(1)) for ref, full in full_weights
+    ]
+    own_weights = [copies.local(ref, rows_of(full, shard)) for ref, full in full_weights]
+
+    far_tokens.wait_recv()
+    partner_rows = span_rows(flipped(ctx, 6, 3))
+    passed_tokens = [
+        copies.send(tokens.at[partner_rows], tokens.at[partner_rows], ctx_peer(offset))
+        for offset in (3, 2, 1)
+    ]
+
+    for copy in local_copies:
+        copy.wait()
+    for copy in head_copies + near_tokens + passed_tokens:
+        copy.wait_recv()
+
+    def full_vec(kind):
+        return jnp.concatenate([vecs[owner, kind : kind + 1, :] for owner in range(4)], axis=1)
+
+    length = len_ref[upper]
+    lane = lax.broadcasted_iota(jnp.int32, (span * 2, LANES), 1)
+
+    def put_query(rows, projected):
+        scaled = (projected + vecs[pair, 0:1, :]).astype(bf16).astype(f32) * (HEAD_DIM**-0.5)
+        q_scaled[rows, :] = scaled.astype(bf16)
+        q_aug[0, rows, :] = jnp.where(
+            lane < HEAD_DIM, scaled, jnp.where(lane == HEAD_DIM, 1.0, 0.0)
+        ).astype(bf16)
+        q_aug[1, rows, :] = jnp.where(
+            lane >= HEAD_DIM, scaled, jnp.where(lane == 0, 1.0, 0.0)
+        ).astype(bf16)
+
+    def put_key_value(rows, key, value, left_out):
+        lanes = lax.broadcasted_iota(jnp.int32, key.shape, 1)
+        key = key.astype(bf16).astype(f32)
+        value = (value + vecs[pair, 1:2, :]).astype(bf16).astype(f32)
+        k_aug[0, rows, :] = jnp.where(
+            lanes < HEAD_DIM, key, jnp.where(lanes == HEAD_DIM, left_out, 0.0)
+        ).astype(bf16)
+        k_aug[1, rows, :] = jnp.where(
+            lanes >= HEAD_DIM, key, jnp.where(lanes == 0, left_out, 0.0)
+        ).astype(bf16)
+        v_mask[0, rows, :] = jnp.where(lanes < HEAD_DIM, value, 0.0).astype(bf16)
+        v_mask[1, rows, :] = jnp.where(lanes >= HEAD_DIM, value, 0.0).astype(bf16)
+        k_turned[:, rows] = key.T.astype(bf16)
+        v_turned[:, rows] = value.T.astype(bf16)
+
+    for block in range(4):
+        rows = pl.ds(block * span * 2, span * 2)
+        projected = matmul(tokens[rows, :], w_heads[...])
+        put_query(rows, projected[:, :LANES])
+        position = block * span * 2 + lax.broadcasted_iota(jnp.int32, (span * 2, LANES), 0)
+        put_key_value(
+            rows,
+            projected[:, LANES : 2 * LANES],
+            projected[:, 2 * LANES :],
+            jnp.where(position < length, 0.0, -1e30),
+        )
+    projected = matmul(mem_ref[upper], w_heads[:, LANES:])
+    position = lax.broadcasted_iota(jnp.int32, (MEM_PAD, LANES), 0)
+    put_key_value(
+        pl.ds(length_all, MEM_PAD),
+        projected[:, :LANES],
+        projected[:, LANES:],
+        jnp.where(position < MEM_ROWS, 0.0, -1e30),
+    )
+
+    att_copies = []
+    for high in (3, 2, 1, 0):
+        block = lax.div(flipped(ctx, 2 * high, 3), 2)
+        rows = pl.ds(pl.multiple_of(block * span * 2, span * 2), span * 2)
+        for head in range(2):
+            scores = back_product(k_aug[head], q_aug[head, rows, :])
+            exponent = jnp.exp(scores - jnp.max(scores, axis=0, keepdims=True))
+            total = jnp.sum(exponent, axis=0, keepdims=True)
+            weights = (exponent * (1.0 / total)).astype(bf16)
+            probs[head, :, rows] = weights
+            half = pl.ds(head * HEAD_DIM, HEAD_DIM)
+            mixed_t[half, rows] = matmul(v_turned[half, :], weights)
+        mixed[rows, :] = mixed_t[:, rows].T.astype(bf16)
+        for low in (0, 1):
+            offset = 2 * high + low
+            source = mixed.at[span_rows(flipped(ctx, offset, 3))]
+            target = att.at[span_rows(upper), pair_lanes(pair)]
+            if offset:
+                att_copies.append(copies.send(source, target, ctx_peer(offset)))
+            else:
+                own_att = copies.local(source, target)
+
+    passed_weights = []
+    for copy, (_, full) in zip(from_x, full_weights):
+        copy.wait_recv()
+        source = rows_of(full, flipped(shard, 2, 2))
+        passed_weights.append(copies.send(source, source, shard_peer(1)))
+    for block in range(4):
+        rows = pl.ds(block * span * 2, span * 2)
+        tokens_t[:, rows] = tokens[rows, :].astype(f32).T.astype(bf16)
+    for copy in own_weights:
+        copy.wait()
+    for copy in from_core + passed_weights:
+        copy.wait_recv()
+    own_att.wait()
+    for copy in att_copies:
+        copy.wait_recv()
+
+    seqs = x_ref.shape[0]
+    local_rows = seqs * span
+    own_x = x_ref[...].reshape(local_rows, width).astype(f32)
+    branch = matmul(att[...], w_out[...]) + full_vec(2)
+    normed, unit_one, inverse_one = norm_forward(own_x + branch, full_vec(4), full_vec(5))
+    normed_low = normed.astype(bf16)
+    ffn_out = jnp.zeros((local_rows, width), f32)
+    for chunk in range(4):
+        columns = pl.ds(chunk * width, width)
+        bias = jnp.concatenate([vecs[chunk, 8 + i : 9 + i, :] for i in range(4)], axis=1)
+        pre_act = matmul(normed_low, w_up[:, columns]) + bias
+        square = pre_act * pre_act
+        bent = jnp.tanh(GELU_SCALE * pre_act * (1.0 + 0.044715 * square))
+        hidden[:, columns] = (0.5 * pre_act * (1.0 + bent)).astype(bf16)
+        act_slope[:, columns] = 0.5 * (1.0 + bent) + 0.5 * pre_act * (1.0 - bent * bent) * (
+            GELU_SCALE * (1.0 + 3 * 0.044715 * square)
+        )
+        ffn_out = ffn_out + matmul(hidden[:, columns], w_down[columns, :])
+    ffn_out = ffn_out + full_vec(3)
+    output, unit_two, inverse_two = norm_forward(normed + ffn_out, full_vec(6), full_vec(7))
+    o_layer[...] = output.astype(bf16)
+
+    cotangent = g_ref[...].reshape(local_rows, width).astype(f32)
+    d_two, grad_second_gain, grad_second_bias = norm_backward(
+        cotangent, unit_two, inverse_two, full_vec(6)
+    )
+    d_ffn = d_two.astype(bf16)
+    d_normed = d_two
+    grads_up_bias = []
+    for chunk in range(4):
+        columns = pl.ds(chunk * width, width)
+        d_hidden = back_product(d_ffn, w_down[columns, :])
+        d_chunk = (d_hidden * act_slope[:, columns]).astype(bf16)
+        d_pre[:, columns] = d_chunk
+        grads_up_bias.append(jnp.sum(d_chunk.astype(f32), axis=0, keepdims=True))
+        d_normed = d_normed + back_product(d_chunk, w_up[:, columns])
+    d_one, grad_first_gain, grad_first_bias = norm_backward(
+        d_normed, unit_one, inverse_one, full_vec(4)
+    )
+    o_input[...] = d_one
+    d_branch = d_one.astype(bf16)
+    d_att[...] = back_product(d_branch, w_out[...]).astype(bf16)
+
+    d_copies = []
+    for offset in (6, 7, 4, 5, 2, 3, 1, 0):
+        peer = flipped(ctx, offset, 3)
+        source = d_att.at[span_rows(lax.div(peer, 4)), pair_lanes(lax.rem(peer, 4))]
+        target = d_mixed.at[span_rows(ctx)]
+        if offset:
+            d_copies.append(copies.send(source, target, ctx_peer(offset)))
+        else:
+            own_d = copies.local(source, target)
+
+    row_id = lax.broadcasted_iota(jnp.int32, (8, LANES), 0)
+    tile = jnp.zeros((8, LANES), f32)
+    for seq in range(seqs):
+        position = ctx * span + lax.broadcasted_iota(jnp.int32, (span, 1), 0)
+        valid = jnp.where(position < len_ref[seq], 1.0, 0.0)
+        for kind, values in enumerate((own_x, branch, ffn_out)):
+            piece = values[seq * span : (seq + 1) * span]
+            row_sum = jnp.sum(piece * piece, axis=1, keepdims=True) * valid
+            tile = tile + jnp.where(
+                row_id == seq * 3 + kind, jnp.sum(row_sum, axis=0, keepdims=True), 0.0
+            )
+    squares[ctx] = tile
+    square_copies = [
+        copies.send(squares.at[ctx], squares.at[ctx], ctx_peer(offset))
+        for offset in (6, 7, 4, 5, 2, 3, 1)
+    ]
+
+    chunks = ((0, width), (width, width), (2 * width, LANES))
+    depth = [dict() for _ in chunks]
+
+    def add_rows(target, first, rows):
+        total = target[...].astype(f32) + first[...].astype(f32)
+        target[...] = total.astype(bf16)
+
+    def core_send(number):
+        start, rows = chunks[number]
+        depth[number]["core"] = [
+            copies.send(
+                partial.at[2 * side + 1 - core, pl.ds(start, rows)],
+                got_core.at[side, pl.ds(start, rows)],
+                shard_peer(1),
+            )
+            for side in range(2)
+        ]
+
+    def x_send(number):
+        start, rows = chunks[number]
+        for side, copy in enumerate(depth[number]["core"]):
+            copy.wait_recv()
+            add_rows(
+                got_core.at[side, pl.ds(start, rows)],
+                partial.at[2 * side + core, pl.ds(start, rows)],
+                rows,
+            )
+        depth[number]["x"] = copies.send(
+            got_core.at[1 - x_half, pl.ds(start, rows)],
+            got_x.at[pl.ds(start, rows)],
+            shard_peer(2),
+        )
+
+    def y_send(number):
+        start, rows = chunks[number]
+        depth[number]["x"].wait_recv()
+        add_rows(got_x.at[pl.ds(start, rows)], got_core.at[x_half, pl.ds(start, rows)], rows)
+        half = rows // 2
+        depth[number]["y"] = copies.send(
+            got_x.at[pl.ds(pl.multiple_of(start + (1 - y_side) * half, half), half)],
+            got_y.at[pl.ds(start // 2, half)],
+            ctx_peer(1),
+        )
+
+    def z_send(number):
+        start, rows = chunks[number]
+        half, quarter = rows // 2, rows // 4
+        depth[number]["y"].wait_recv()
+        add_rows(
+            got_y.at[pl.ds(start // 2, half)],
+            got_x.at[pl.ds(pl.multiple_of(start + y_side * half, half), half)],
+            half,
+        )
+        depth[number]["z"] = copies.send(
+            got_y.at[
+                pl.ds(pl.multiple_of(start // 2 + (1 - z_side) * quarter, quarter), quarter)
+            ],
+            got_z.at[pl.ds(start // 4, quarter)],
+            ctx_peer(2),
+        )
+
+    def far_send(number):
+        start, rows = chunks[number]
+        quarter = rows // 4
+        depth[number]["z"].wait_recv()
+        add_rows(
+            got_z.at[pl.ds(start // 4, quarter)],
+            got_y.at[pl.ds(pl.multiple_of(start // 2 + z_side * quarter, quarter), quarter)],
+            quarter,
+        )
+        depth[number]["far"] = copies.send(
+            got_z.at[pl.ds(start // 4, quarter)],
+            got_far.at[pl.ds(start // 4, quarter)],
+            ctx_peer(6),
+        )
+
+    def z_gather(number):
+        start, rows = chunks[number]
+        half, quarter = rows // 2, rows // 4
+        depth[number]["far"].wait_recv()
+        place = pl.ds(pl.multiple_of(start + y_side * half + z_side * quarter, quarter), quarter)
+        here = pl.ds(start // 4, quarter)
+        final[place, :] = (got_z[here, :].astype(f32) + got_far[here, :].astype(f32)).astype(bf16)
+        depth[number]["z gather"] = copies.send(final.at[place], final.at[place], ctx_peer(2))
+
+    def y_gather(number):
+        start, rows = chunks[number]
+        half = rows // 2
+        depth[number]["z gather"].wait_recv()
+        place = pl.ds(pl.multiple_of(start + y_side * half, half), half)
+        depth[number]["y gather"] = copies.send(final.at[place], final.at[place], ctx_peer(1))
+
+    for owner in range(4):
+        partial[owner, :width, :] = outer_sum(
+            hidden[:, owner * width : (owner + 1) * width], d_ffn
+        ).astype(bf16)
+    core_send(0)
+    for chunk in range(4):
+        grad_up = outer_sum(normed_low, d_pre[:, chunk * width : (chunk + 1) * width]).astype(bf16)
+        for owner in range(4):
+            partial[owner, width + chunk * LANES : width + (chunk + 1) * LANES, :] = grad_up[
+                owner * LANES : (owner + 1) * LANES
+            ]
+    core_send(1)
+    grad_out = outer_sum(att[...], d_branch).astype(bf16)
+    for owner in range(4):
+        partial[owner, 2 * width :, :] = grad_out[owner * LANES : (owner + 1) * LANES]
+    core_send(2)
+    x_send(0)
+    x_send(1)
+    x_send(2)
+
+    grad_down_bias = jnp.sum(d_ffn.astype(f32), axis=0, keepdims=True)
+    grad_out_bias = jnp.sum(d_branch.astype(f32), axis=0, keepdims=True)
+    vec_part[...] = jnp.zeros_like(vec_part)
+    wide_grads = (
+        grad_out_bias,
+        grad_down_bias,
+        grad_first_gain,
+        grad_first_bias,
+        grad_second_gain,
+        grad_second_bias,
+    )
+    for owner in range(4):
+        for kind, values in enumerate(wide_grads):
+            vec_part[owner, 2 + kind : 3 + kind, :] = values.reshape(1, width)[
+                :, owner * LANES : (owner + 1) * LANES
+            ]
+        for piece in range(4):
+            vec_part[owner, 8 + piece : 9 + piece, :] = grads_up_bias[owner][
+                :, piece * LANES : (piece + 1) * LANES
+            ]
+
+    own_d.wait()
+    for copy in d_copies:
+        copy.wait_recv()
+    d_turned = d_mixed[...].astype(f32).T * mixed_t[...]
+    for head in range(2):
+        half = slice(head * HEAD_DIM, (head + 1) * HEAD_DIM)
+        delta = jnp.sum(d_turned[half], axis=0, keepdims=True)
+        for block in range(4):
+            rows = slice(block * span * 2, (block + 1) * span * 2)
+            dots = back_product(v_mask[head], d_mixed[rows, :])
+            weights = probs[head, :, rows].astype(f32)
+            d_scores[head, :, rows] = (weights * (dots - delta[:, rows])).astype(bf16)
+    y_send(0)
+    key_lane = lax.broadcasted_iota(jnp.int32, (keys, LANES), 1)
+    grad_value = jnp.where(
+        key_lane < HEAD_DIM, matmul(probs[0], d_mixed[...]), matmul(probs[1], d_mixed[...])
+    ).astype(bf16)
+    grad_key = jnp.where(
+        key_lane < HEAD_DIM, matmul(d_scores[0], q_scaled[...]), matmul(d_scores[1], q_scaled[...])
+    ).astype(bf16)
+    grad_query = jnp.concatenate(
+        [
+            matmul(k_turned[:HEAD_DIM, :], d_scores[0]),
+            matmul(k_turned[HEAD_DIM:, :], d_scores[1]),
+        ],
+        axis=0,
+    ) * (HEAD_DIM**-0.5)
+    grad_query = grad_query.T.astype(bf16)
+    joined = jnp.concatenate([grad_query, grad_key[:length_all], grad_value[:length_all]], axis=1)
+    mem_joined = jnp.concatenate([grad_key[length_all:], grad_value[length_all:]], axis=1)
+
+    for block in range(4):
+        rows = slice(block * span * 2, (block + 1) * span * 2)
+        dx_part[rows, :] = back_product(joined[rows], w_heads[...]).astype(bf16)
+    dx_copies = [[], []]
+    for order, mirror in enumerate((6, 0)):
+        for offset in (3, 2, 1):
+            source = dx_part.at[span_rows(flipped(ctx, offset ^ mirror, 3))]
+            dx_copies[order].append(
+                copies.send(source, dx_got.at[order, offset - 1], ctx_peer(offset))
+            )
+    mem_part[pair] = back_product(mem_joined, w_heads[:, LANES:]).astype(bf16)
+    mem_copies = [
+        copies.send(mem_part.at[pair], mem_part.at[pair], ctx_peer(offset)) for offset in (3, 2, 1)
+    ]
+    y_send(1)
+
+    grad_heads = matmul(tokens_t[...], joined)
+    mem_grad = outer_sum(mem_ref[upper], mem_joined)
+    for owner in range(4):
+        rows = slice(owner * LANES, (owner + 1) * LANES)
+        head_part[owner, :LANES, :LANES] = grad_heads[rows, :LANES].astype(bf16)
+        head_part[owner, :LANES, LANES:] = (grad_heads[rows, LANES:] + mem_grad[rows]).astype(bf16)
+    query_bias = jnp.sum(grad_query.astype(f32), axis=0, keepdims=True)
+    value_bias = jnp.sum(grad_value.astype(f32), axis=0, keepdims=True)
+    for owner in range(4):
+        mine = pair == owner
+        vec_part[owner, 0:1, :] = jnp.where(mine, query_bias, 0.0)
+        vec_part[owner, 1:2, :] = jnp.where(mine, value_bias, 0.0)
+        head_part[owner, LANES:, :] = jnp.zeros((ROW_KINDS, 3 * LANES), bf16)
+        head_part[owner, LANES:, :LANES] = vec_part[owner].astype(bf16)
+    head_core_copies = [
+        copies.send(head_part.at[2 * side + 1 - core], head_core.at[side], shard_peer(1))
+        for side in range(2)
+    ]
+    y_send(2)
+    z_send(0)
+    for side, copy in enumerate(head_core_copies):
+        copy.wait_recv()
+        add_rows(head_core.at[side], head_part.at[2 * side + core], LANES)
+    head_x_copy = copies.send(head_core.at[1 - x_half], head_x, shard_peer(2))
+    z_send(1)
+
+    for copy in dx_copies[0]:
+        copy.wait_recv()
+    far_rows = span_rows(flipped(ctx, 6, 3))
+    dx_far_sum[...] = (
+        dx_part[far_rows, :].astype(f32)
+        + dx_got[0, 0].astype(f32)
+        + dx_got[0, 1].astype(f32)
+        + dx_got[0, 2].astype(f32)
+    ).astype(bf16)
+    dx_far_copy = copies.send(dx_far_sum, dx_far, ctx_peer(6))
+    for copy in mem_copies:
+        copy.wait_recv()
+    mem_far[upper] = (
+        mem_part[0].astype(f32)
+        + mem_part[1].astype(f32)
+        + mem_part[2].astype(f32)
+        + mem_part[3].astype(f32)
+    ).astype(bf16)
+    mem_far_copy = copies.send(mem_far.at[upper], mem_far.at[upper], ctx_peer(6))
+    head_x_copy.wait_recv()
+    add_rows(head_x, head_core.at[x_half], LANES)
+    head_far_copy = copies.send(head_x, head_far, ctx_peer(4))
+    z_send(2)
+    far_send(0)
+    far_send(1)
+    far_send(2)
+
+    for copy in dx_copies[1]:
+        copy.wait_recv()
+    near = pl.ds(pl.multiple_of(upper * span, span), span)
+    o_input[near, :] = (
+        o_input[near, :]
+        + dx_part[span_rows(ctx), :].astype(f32)
+        + dx_got[1, 0].astype(f32)
+        + dx_got[1, 1].astype(f32)
+        + dx_got[1, 2].astype(f32)
+    )
+    head_far_copy.wait_recv()
+    head_all[pair] = (head_x[...].astype(f32) + head_far[...].astype(f32)).astype(bf16)
+    head_copies = [
+        copies.send(head_all.at[pair], head_all.at[pair], ctx_peer(offset)) for offset in (3, 2, 1)
+    ]
+    z_gather(0)
+    z_gather(1)
+    z_gather(2)
+    dx_far_copy.wait_recv()
+    far = pl.ds(pl.multiple_of((1 - upper) * span, span), span)
+    o_input[far, :] = o_input[far, :] + dx_far[...].astype(f32)
+    mem_far_copy.wait_recv()
+    o_mem[...] = mem_far[...].astype(f32)
+    for copy in square_copies:
+        copy.wait_recv()
+    total = squares[0]
+    for other in range(1, spans):
+        total = total + squares[other]
+    valid_tokens = jnp.where(row_id < 3, len_ref[0], len_ref[1]).astype(f32)
+    o_rms[...] = jnp.sqrt(total / (valid_tokens * width))
+    y_gather(0)
+    y_gather(1)
+    y_gather(2)
+    for copy in head_copies:
+        copy.wait_recv()
+    for owner in range(4):
+        for part in range(3):
+            o_qkv[part, :, owner * LANES : (owner + 1) * LANES] = head_all[
+                owner, :LANES, part * LANES : (part + 1) * LANES
+            ]
+    o_vec[...] = (
+        head_all[0, LANES:, :LANES].astype(f32)
+        + head_all[1, LANES:, :LANES].astype(f32)
+        + head_all[2, LANES:, :LANES].astype(f32)
+        + head_all[3, LANES:, :LANES].astype(f32)
+    )
+    for number in range(len(chunks)):
+        depth[number]["y gather"].wait_recv()
+    o_fin[...] = final[...]
+    copies.finish()
+
+
+def fast_layer(
+    inputs,
+    memory,
+    lengths,
+    w_query,
+    w_key,
+    w_value,
+    w_out,
+    w_up,
+    w_down,
+    b_query,
+    b_value,
+    b_out,
+    b_up,
+    b_down,
+    first_gain,
+    first_bias,
+    second_gain,
+    second_bias,
+    out_grad,
+):
+    bf16, f32 = jnp.bfloat16, jnp.float32
+    seqs, span, width = inputs.shape
+    length_all, keys = 8 * span, 8 * span + MEM_PAD
+    hidden_width = w_up.shape[1]
+    vec = jnp.concatenate(
+        [
+            jnp.stack(
+                [
+                    b_query,
+                    b_value,
+                    b_out,
+                    b_down,
+                    first_gain,
+                    first_bias,
+                    second_gain,
+                    second_bias,
+                ]
+            ),
+            b_up.reshape(4, LANES),
+            jnp.zeros((4, LANES), bf16),
+        ]
+    ).astype(f32)
+    padded = jnp.pad(memory, ((0, 0), (0, MEM_PAD - memory.shape[1]), (0, 0)))
+    vmem, anywhere = pl.BlockSpec(memory_space=pltpu.VMEM), pl.BlockSpec(memory_space=pl.ANY)
+    smem = pl.BlockSpec(memory_space=pltpu.SMEM)
+    stacked = 2 * width + LANES
+    scratch = [
+        ((length_all, width), bf16),
+        ((width, length_all), bf16),
+        ((width, 3 * LANES), bf16),
+        ((width, width), bf16),
+        ((width, hidden_width), bf16),
+        ((hidden_width, width), bf16),
+        ((4, ROW_KINDS, LANES), f32),
+        ((length_all, LANES), bf16),
+        ((2, length_all, LANES), bf16),
+        ((2, keys, LANES), bf16),
+        ((2, keys, LANES), bf16),
+        ((LANES, keys), bf16),
+        ((LANES, keys), bf16),
+        ((2, keys, length_all), bf16),
+        ((2, keys, length_all), bf16),
+        ((LANES, length_all), f32),
+        ((length_all, LANES), bf16),
+        ((seqs * span, width), bf16),
+        ((seqs * span, hidden_width), bf16),
+        ((seqs * span, hidden_width), f32),
+        ((seqs * span, hidden_width), bf16),
+        ((seqs * span, width), bf16),
+        ((length_all, LANES), bf16),
+        ((4, stacked, width), bf16),
+        ((2, stacked, width), bf16),
+        ((stacked, width), bf16),
+        ((stacked // 2, width), bf16),
+        ((stacked // 4, width), bf16),
+        ((stacked // 4, width), bf16),
+        ((stacked, width), bf16),
+        ((4, LANES + ROW_KINDS, 3 * LANES), bf16),
+        ((2, LANES + ROW_KINDS, 3 * LANES), bf16),
+        ((LANES + ROW_KINDS, 3 * LANES), bf16),
+        ((LANES + ROW_KINDS, 3 * LANES), bf16),
+        ((4, LANES + ROW_KINDS, 3 * LANES), bf16),
+        ((4, ROW_KINDS, LANES), f32),
+        ((length_all, width), bf16),
+        ((2, 3, span, width), bf16),
+        ((span, width), bf16),
+        ((span, width), bf16),
+        ((4, MEM_PAD, width), bf16),
+        ((2, MEM_PAD, width), bf16),
+        ((8, 8, LANES), f32),
+    ]
+    layer, input_grad, mem_grad, weight_grads, head_grads, vec_grads, rms = pl.pallas_call(
+        layer_kernel,
+        out_shape=[
+            jax.ShapeDtypeStruct((seqs * span, width), bf16),
+            jax.ShapeDtypeStruct((seqs * span, width), f32),
+            jax.ShapeDtypeStruct((2, MEM_PAD, width), f32),
+            jax.ShapeDtypeStruct((stacked, width), bf16),
+            jax.ShapeDtypeStruct((3, LANES, width), bf16),
+            jax.ShapeDtypeStruct((ROW_KINDS, LANES), f32),
+            jax.ShapeDtypeStruct((8, LANES), f32),
+        ],
+        in_specs=[vmem, vmem, vmem, smem, vmem] + [anywhere] * 6,
+        out_specs=[vmem] * 7,
+        scratch_shapes=[pltpu.VMEM(shape, kind) for shape, kind in scratch]
+        + [pltpu.SemaphoreType.DMA((SLOTS,)), pltpu.SemaphoreType.DMA((SLOTS,))],
+        compiler_params=pltpu.CompilerParams(
+            collective_id=0, has_side_effects=True, vmem_limit_bytes=60 * 2**20
+        ),
+        name="layer",
+    )(inputs, out_grad, padded, lengths, vec, w_query, w_key, w_value, w_out, w_up, w_down)
+    return (
+        layer.reshape(seqs, span, width),
+        input_grad.reshape(seqs, span, width),
+        mem_grad[:, : memory.shape[1]],
+        head_grads[0].astype(f32),
+        head_grads[1].astype(f32),
+        head_grads[2].astype(f32),
+        weight_grads[2 * width :].astype(f32),
+        weight_grads[width : 2 * width]
+        .reshape(4, LANES, width)
+        .transpose(1, 0, 2)
+        .reshape(LANES, hidden_width)
+        .astype(f32),
+        weight_grads[:width].astype(f32),
+        vec_grads[0],
+        vec_grads[1],
+        vec_grads[2],
+        vec_grads[8:12].reshape(4 * LANES),
+        vec_grads[3],
+        vec_grads[4],
+        vec_grads[5],
+        vec_grads[6],
+        vec_grads[7],
+        rms[:6, 0].reshape(2, 3),
+    )
+
+
+def takes_fast_plan(mesh, inputs, memory, w_up):
+    return (
+        mesh.shape["shard"] == 4
+        and mesh.shape["ctx"] == 8
+        and inputs.shape == (2, LANES, HEADS * HEAD_DIM)
+        and memory.shape[1] == MEM_ROWS
+        and w_up.shape == (LANES, 4 * HEADS * HEAD_DIM)
+    )
+
+
 def solution(mesh):
     in_specs = (
         P("shard", "ctx", None),
@@ -578,4 +1370,10 @@
         P("shard"),
         P("shard", None),
     )
-    return jax.shard_map(local, mesh=mesh, in_specs=in_specs, out_specs=out_specs, check_vma=False)
+
+    def layer(*arrays):
+        if takes_fast_plan(mesh, arrays[0], arrays[1], arrays[7]):
+            return fast_layer(*arrays)
+        return local(*arrays)
+
+    return jax.shard_map(layer, mesh=mesh, in_specs=in_specs, out_specs=out_specs, check_vma=False)

time: 581 us -> 143 us (0.25)
  blocking collectives: 324 us -> 0 us
  Pallas kernels: 0 us -> 125 us
  waiting for transfers between devices: 103 us -> 0 us
  matrix products: 74.5 us -> 0 us
  local copies, waits for them, and re-layouts: 43.1 us -> 11.3 us
  between operations: 16.8 us -> 0.7 us
  other arithmetic: 12.6 us -> 5.59 us
    psum x2 -> x0, blocking collectives: 173 us -> none  [the longest x1 131 us: local(): lax.psum((part_query, part_key, part_value, part_out, part_up, part_down,...]
    all_gather x15 -> x0, blocking collectives: 142 us -> none  [the longest x1 32.4 us: local(): lax.all_gather(log_total, 'ctx', axis=1, tiled=True)]
    pallas_call x0 -> x1, Pallas kernels: none -> 125 us  [fast_layer(): pl.pallas_call(layer_kernel, out_shape=[jax.ShapeDtypeStruct((seqs * span...]
    dot_general x36 -> x0, matrix products: 74.5 us -> none  [the longest x8 11.9 us: matmul(): return jnp.dot(operand, second, preferred_element_type=jnp.float32)]
    unnamed x15 -> x0, waiting for transfers between devices: 50.5 us -> none
    all_gather x6 -> x0, waiting for transfers between devices: 38.8 us -> none  [the longest x1 20.4 us: local(): lax.all_gather(w_down, 'shard', axis=0, tiled=True)]
    all_gather x4 -> x0, local copies, waits for them, and re-layouts: 15.5 us -> none  [the longest x1 4.41 us: local(): lax.all_gather(grad_att, 'ctx', axis=1, tiled=True)]
    unnamed x140 -> x10, local copies, waits for them, and re-layouts: 18.1 us -> 2.99 us
  transfers between devices with their start and end apart: 12 -> 0, of which waited for: 6 -> 0; matrix products, arithmetic and copies ran while one was open for 21% -> 0% of each run, Pallas kernels for 0% -> 0%
where the time goes in v1:
time: 143 us
  Pallas kernels  125 us (87%)
  local copies, waits for them, and re-layouts  11.3 us (8%)
  other arithmetic  5.59 us (4%)
    pallas_call x1, Pallas kernels, fast_layer(): pl.pallas_call(layer_kernel, out_shape=[jax.ShapeDtypeStruct((seqs * span...  125 us
    unnamed x10, local copies, waits for them, and re-layouts  2.99 us

profile of v1, /device:TPU:0, one launch (start us, length us, event | category | flops | bytes accessed | tf_op | source)
XLA Modules:
  0.0 143.0 jit_solution(10248518811323236717)
XLA Ops:
  0.7 1.5 %concatenate.3 = bf16[16,128]{1,0:T(8,128)(2,1)S(1)} concatenate(bf16[1,128]{1,0:T(2,128)(2,1)} %bitcast.49, bf16[1,128]{1,0:T(2,128)(2,1)} %bitcast.50, bf16[1,128]{1,0:T(2,128)(2,1)} %bitcast.51, bf16[1,128]{1,0:T(2,128)(2,1)} %bitcast.52, bf16[1,128]{1,0:T(2,128)(2,1)} %bitcast.53, bf16[1,128]{1,0:T(2,128)(2,1)} %bitcast.54, bf16[1,128]{1,0:T(2,128)(2,1)} %bitcast.55, ...), dimensions={0} | concatenate | bytes 8192 | tf_op jit(solution)/shard_map/concatenate | solution.py:1206
  2.2 0.6 convert_element_type.41.vec_ref
  2.8 0.8 copy.41
  3.6 0.6 pad.4.mem_ref
  4.2 125.4 %layer.1 = (bf16[256,512]{1,0:T(8,128)(2,1)}, f32[256,512]{1,0:T(8,128)}, f32[2,32,512]{2,1,0:T(8,128)}, bf16[1152,512]{1,0:T(8,128)(2,1)}, bf16[3,128,512]{2,1,...) custom-call(bf16[2,128,512]{2,1,0:T(8,128)(2,1)} %x_ref.1, bf16[2,128,512]{2,1,0:T(8,128)(2,1)} %g_ref.1, ...), custom_call_target="tpu_custom_call" | custom-call | tf_op jit(solution)/shard_map/layer/pallas_call | solution.py:1273
  129.6 0.8 slice_reduce_fusion
  130.4 0.6 reshape_squeeze.3
  131.0 1.3 slice_bitcast_fusion
  132.3 1.5 %slice_bitcast_fusion.1 = (f32[128]{0:T(128)}, f32[128]{0:T(128)}, f32[128]{0:T(128)}, f32[128]{0:T(128)}, f32[128]{0:T(128)}, /*index=5*/f32[128]{0:T(128)}, f32[128]{0:T(128)}, f32[128]{0:T(128)}) fusion(f32[16,128]{1,0:T(8,128)} %get-tuple-element.31), kind=kLoop, calls=%fused_computation.8 | loop fusion | bytes 8192 | tf_op jit(solution)/shard_map/squeeze | solution.py:1315
  133.8 0.9 slice.51
  134.7 0.7 copy.43
  135.4 1.6 %slice_convert_fusion.1 = f32[128,512]{1,0:T(8,128)} fusion(bf16[1152,512]{1,0:T(8,128)(2,1)} %get-tuple-element.30), kind=kLoop, calls=%fused_computation.5 | loop fusion | flops 65536 | bytes 393216 | tf_op jit(solution)/shard_map/convert_element_type | solution.py:1300
  137.0 2.3 %slice_convert_fusion = (f32[512,512]{1,0:T(8,128)}, bf16[512,512]{1,0:T(8,128)(2,1)S(1)}) fusion(bf16[1152,512]{1,0:T(8,128)(2,1)} %get-tuple-element.30), kind=kLoop, calls=%fused_computation.1 | loop fusion | flops 262144 | bytes 2621440 | tf_op jit(solution)/shard_map/convert_element_type | solution.py:1306
  139.3 0.1 convert_bitcast_fusion
  139.5 0.0 copy-start.1
  139.5 0.0 copy-start.2
  139.5 1.1 copy.44
  140.6 0.0 copy-start
  140.6 0.0 copy-done.1
  140.6 0.9 bitcast_convert_fusion
  141.5 0.0 copy-done.2
  141.5 0.7 copy.47
  142.2 0.0 copy-done
  142.2 0.8 copy.48
  (1 shorter events, 0.0 us)
Async XLA Ops:
  139.5 1.1 copy-start.1
  139.5 2.0 %copy-start.2 = (bf16[256,512]{1,0:T(8,128)(2,1)S(1)}, bf16[256,512]{1,0:T(8,128)(2,1)}, u32[]{:S(2)}) copy-start(bf16[256,512]{1,0:T(8,128)(2,1)} %get-tuple-element.26) | copy-start | bytes 786436
  140.6 1.6 %copy-start = (f32[256,512]{1,0:T(8,128)S(1)}, f32[256,512]{1,0:T(8,128)}, u32[]{:S(2)}) copy-start(f32[256,512]{1,0:T(8,128)} %get-tuple-element.27) | copy-start | bytes 1572868

commit v2 on v0

--- a/solution.py
+++ b/solution.py
@@ -3,10 +3,14 @@
 import jax
 import jax.numpy as jnp
 from jax import lax
+from jax.experimental import pallas as pl
+from jax.experimental.pallas import tpu as pltpu
 from jax.sharding import PartitionSpec as P
 
 HEADS = 8
 HEAD_DIM = 64
+MEM_ROWS = 20
+GELU_SCALE = math.sqrt(2 / math.pi)
 
 
 eps = 1e-05
@@ -535,6 +539,1193 @@
     )
 
 
+MESH_ID = pl.DeviceIdType.MESH
+LANES = 128
+MEM_PAD = 32
+ROW_KINDS = 16
+SENDS, ARRIVALS, KEPT = 18, 87, 23
+PIECES = ((128, 'xyz'), (128, 'zyx'), (128, 'yxz'), (128, 'yxz'), (256, 'xyz'), (256, 'zyx'), (128, 'yzx'))
+
+
+def flipped(index, offset, bits):
+    total = 0
+    for bit in range(bits):
+        digit = lax.rem(lax.div(index, 2**bit), 2)
+        if offset >> bit & 1:
+            digit = 1 - digit
+        total = total + digit * 2**bit
+    return total
+
+
+class Copies:
+    def __init__(self, send_sems, recv_sems, local_sems, measure):
+        self.send_sems, self.recv_sems, self.local_sems = send_sems, recv_sems, local_sems
+        self.measure = measure
+        self.sent, self.alone, self.received, self.kept = [], [], 0, 0
+
+    def send(self, src, dst, device):
+        return self.send_all([(src, dst, device)], dst)
+
+    def send_all(self, items, whole):
+        rows = math.prod(whole.shape) * whole.dtype.itemsize // (2 * self.measure.shape[1])
+        if rows % 16:
+            pool = len(self.sent)
+            self.sent.append(None)
+            self.alone.append((pool, whole))
+        else:
+            pool = next(
+                (
+                    number
+                    for number, held in enumerate(self.sent)
+                    if held is not None and held + rows <= self.measure.shape[0]
+                ),
+                len(self.sent),
+            )
+            if pool == len(self.sent):
+                self.sent.append(0)
+            self.sent[pool] += rows
+        arrival = self.recv_sems.at[self.received]
+        self.received += 1
+        for src, dst, device in items:
+            pltpu.make_async_remote_copy(
+                src_ref=src,
+                dst_ref=dst,
+                send_sem=self.send_sems.at[pool],
+                recv_sem=arrival,
+                device_id=device,
+                device_id_type=MESH_ID,
+            ).start()
+        return Arrival(whole, arrival)
+
+    def keep(self, items, whole):
+        done = self.local_sems.at[self.kept]
+        self.kept += 1
+        for src, dst in items:
+            pltpu.make_async_copy(src, dst, done).start()
+        return Arrival(whole, done)
+
+    def finish(self):
+        for pool, whole in self.alone:
+            Arrival(whole, self.send_sems.at[pool]).wait()
+        for pool, rows in enumerate(self.sent):
+            if rows is not None:
+                Arrival(self.measure.at[pl.ds(0, rows)], self.send_sems.at[pool]).wait()
+
+
+class Held:
+    pass
+
+
+class Arrival:
+    def __init__(self, whole, semaphore):
+        self.whole, self.semaphore = whole, semaphore
+
+    def wait(self):
+        pltpu.make_async_copy(self.whole, self.whole, self.semaphore).wait()
+
+
+def layer_kernel(
+    x_ref,
+    g_ref,
+    mem_ref,
+    len_ref,
+    wq_ref,
+    wk_ref,
+    wv_ref,
+    wo_ref,
+    wu_ref,
+    wd_ref,
+    *refs,
+):
+    vec_refs, refs = refs[:9], refs[9:]
+    (o_layer, o_input, o_mem, o_fin, o_heads, o_rms), refs = refs[:6], refs[6:]
+    (
+        own_in,
+        own_g,
+        own_mem,
+        mem_in,
+        *rest,
+    ) = refs
+    narrow_in, rest = rest[:8], rest[8:]
+    (
+        wide_in,
+        rms_rows,
+        d_branch,
+        joined,
+        out_rows,
+        in_grad,
+        tokens,
+        tokens_t,
+        w_heads,
+        w_out,
+        w_up,
+        w_down,
+        vecs,
+        q_scaled,
+        q_aug,
+        k_aug,
+        v_mask,
+        k_turned,
+        v_turned,
+        probs,
+        d_scores,
+        mixed_t,
+        inverse_total,
+        d_scaled,
+        d_scaled_t,
+        mixed,
+        att,
+        hidden,
+        act_slope,
+        d_pre,
+        d_att,
+        d_mixed,
+        partial,
+        got_core,
+        got_first,
+        got_second,
+        got_third,
+        got_far,
+        final,
+        head_part,
+        head_core,
+        head_x,
+        head_far,
+        head_all,
+        vec_part,
+        dx_part,
+        dx_got,
+        dx_far,
+        mem_part,
+        mem_far,
+        squares,
+        send_sems,
+        recv_sems,
+        local_sems,
+    ) = rest
+    bf16, f32 = jnp.bfloat16, jnp.float32
+    shard, ctx = lax.axis_index("shard"), lax.axis_index("ctx")
+    span, width = x_ref.shape[1], x_ref.shape[2]
+    spans = 8
+    length_all = span * spans
+    keys = length_all + MEM_PAD
+    x_half, core = lax.div(shard, 2), lax.rem(shard, 2)
+    upper, pair = lax.div(ctx, 4), lax.rem(ctx, 4)
+    y_side = lax.rem(ctx, 2)
+    z_side = lax.rem(lax.div(ctx, 2) + upper, 2)
+
+    def shard_peer(offset):
+        return {"shard": flipped(shard, offset, 2), "ctx": ctx}
+
+    def ctx_peer(offset):
+        return {"shard": shard, "ctx": flipped(ctx, offset, 3)}
+
+    def span_rows(index):
+        return pl.ds(pl.multiple_of(index * span, span), span)
+
+    def pair_lanes(index, size=LANES):
+        return pl.ds(pl.multiple_of(index * LANES, LANES), size)
+
+    copies = Copies(send_sems, recv_sems, local_sems, partial.at[0])
+
+    barrier = pltpu.get_barrier_semaphore()
+    for offset in (1, 2, 3):
+        pl.semaphore_signal(barrier, inc=1, device_id=shard_peer(offset), device_id_type=MESH_ID)
+    for offset in range(1, 8):
+        pl.semaphore_signal(barrier, inc=1, device_id=ctx_peer(offset), device_id_type=MESH_ID)
+
+    def rows_of(ref, index, start=0, rows=None):
+        owned = ref.shape[0] // 4
+        return ref.at[pl.ds(pl.multiple_of(index * owned + start, LANES), rows or owned)]
+
+    my_rows = pl.ds(pl.multiple_of(shard * LANES, LANES), LANES)
+    head_refs = (wq_ref, wk_ref, wv_ref)
+    own_blocks = [
+        copies.keep(
+            [
+                (
+                    ref.at[:, pair_lanes(pair)],
+                    w_heads.at[my_rows, pl.ds(part * LANES, LANES)],
+                )
+                for part, ref in enumerate(head_refs)
+            ],
+            w_heads.at[my_rows],
+        ),
+        copies.keep([(x_ref.at[upper], tokens.at[span_rows(ctx)])], own_in.at[0]),
+    ]
+    narrow_copies = [
+        copies.keep([(ref, copied)], copied)
+        for ref, copied in zip(vec_refs, (*narrow_in, wide_in))
+    ]
+    full_weights = ((wo_ref, w_out), (wd_ref, w_down), (wu_ref, w_up))
+    own_weights = [
+        copies.keep([(ref, rows_of(full, shard)) for ref, full in full_weights], partial.at[0]),
+        copies.keep([(x_ref, own_in)], own_in),
+        copies.keep([(g_ref, own_g)], own_g),
+        copies.keep([(mem_ref, mem_in)], mem_in),
+    ]
+    pl.semaphore_wait(barrier, 10)
+
+    partner = flipped(ctx, 6, 3)
+    half_span = span // 2
+
+    def half_rows(index, half):
+        return pl.ds(pl.multiple_of(index * span + half * half_span, half_span), half_span)
+
+    far_tokens = [
+        copies.send(
+            x_ref.at[1 - upper, pl.ds(half * half_span, half_span)],
+            tokens.at[half_rows(ctx, half)],
+            ctx_peer(6),
+        )
+        for half in range(2)
+    ]
+    def near_send(offsets):
+        return copies.send_all(
+            [
+                (x_ref.at[upper], tokens.at[span_rows(ctx)], ctx_peer(offset))
+                for offset in offsets
+            ],
+            tokens.at[pl.ds(0, span * len(offsets))],
+        )
+
+    near_pair, near_y = near_send((3, 2)), near_send((1,))
+
+    def send_head_rows(offset):
+        return copies.send_all(
+            [
+                (
+                    ref.at[:, pair_lanes(pair)],
+                    w_heads.at[my_rows, pl.ds(part * LANES, LANES)],
+                    shard_peer(offset),
+                )
+                for part, ref in enumerate(head_refs)
+            ],
+            w_heads.at[my_rows],
+        )
+
+    x_heads = send_head_rows(2)
+    core_heads = send_head_rows(1)
+    for copy in narrow_copies:
+        copy.wait()
+    for kind, ref in enumerate((*narrow_in, wide_in)):
+        values = ref[...].astype(f32)
+        for piece in range(ref.shape[0] // LANES):
+            vecs[shard, kind + piece : kind + piece + 1, :] = values[
+                piece * LANES : (piece + 1) * LANES
+            ].reshape(1, LANES)
+    vec_copies = copies.send_all(
+        [(vecs.at[shard], vecs.at[shard], shard_peer(offset)) for offset in (2, 3, 1)],
+        vecs.at[pl.ds(0, 3)],
+    )
+    half_down = wd_ref.shape[0] // 2
+    x_out = copies.send(wo_ref, rows_of(w_out, shard), shard_peer(2))
+    x_down = copies.send(
+        wd_ref.at[pl.ds(pl.multiple_of(y_side * half_down, LANES), half_down)],
+        rows_of(w_down, shard, y_side * half_down, half_down),
+        shard_peer(2),
+    )
+    x_up = copies.send(wu_ref, rows_of(w_up, shard), shard_peer(2))
+    core_weights = copies.send_all(
+        [(ref, rows_of(full, shard), shard_peer(1)) for ref, full in full_weights], partial.at[0]
+    )
+
+    for copy in own_weights:
+        copy.wait()
+    own_mem[...] = jnp.zeros_like(own_mem)
+    for seq in range(own_mem.shape[0]):
+        own_mem[seq, :MEM_ROWS, :] = mem_in[:, seq, :]
+
+    passed_pair, passed_y = [], []
+    for half, copy in enumerate(far_tokens):
+        copy.wait()
+        place = tokens.at[half_rows(partner, half)]
+        passed_pair.append(
+            copies.send_all(
+                [(place, place, ctx_peer(3)), (place, place, ctx_peer(2))], tokens.at[pl.ds(0, span)]
+            )
+        )
+        passed_y.append(copies.send(place, place, ctx_peer(1)))
+    x_heads.wait()
+    x_owner = flipped(shard, 2, 2)
+    place = rows_of(w_heads, x_owner)
+    passed_heads = copies.send(place, place, shard_peer(1))
+    x_out.wait()
+    x_down.wait()
+    place = rows_of(w_down, x_owner, y_side * half_down, half_down)
+    y_down = copies.send(place, place, ctx_peer(1))
+    passed_early = copies.send_all(
+        [(part, part, shard_peer(1)) for part in (rows_of(w_out, x_owner), place)],
+        partial.at[0, pl.ds(0, LANES + half_down)],
+    )
+
+    for copy in own_blocks:
+        copy.wait()
+    for copy in (core_heads, passed_heads, vec_copies):
+        copy.wait()
+
+    def full_vec(kind):
+        return jnp.concatenate([vecs[owner, kind : kind + 1, :] for owner in range(4)], axis=1)
+
+    length = len_ref[upper]
+    lane = lax.broadcasted_iota(jnp.int32, (span * 2, LANES), 1)
+
+    def put_query(rows, projected):
+        scaled = (projected + vecs[pair, 0:1, :]).astype(bf16).astype(f32) * (HEAD_DIM**-0.5)
+        q_scaled[rows, :] = scaled.astype(bf16)
+        q_aug[0, rows, :] = jnp.where(
+            lane < HEAD_DIM, scaled, jnp.where(lane == HEAD_DIM, 1.0, 0.0)
+        ).astype(bf16)
+        q_aug[1, rows, :] = jnp.where(
+            lane >= HEAD_DIM, scaled, jnp.where(lane == 0, 1.0, 0.0)
+        ).astype(bf16)
+
+    def put_key_value(rows, key, value, left_out):
+        lanes = lax.broadcasted_iota(jnp.int32, key.shape, 1)
+        key = key.astype(bf16).astype(f32)
+        value = (value + vecs[pair, 1:2, :]).astype(bf16).astype(f32)
+        k_aug[0, rows, :] = jnp.where(
+            lanes < HEAD_DIM, key, jnp.where(lanes == HEAD_DIM, left_out, 0.0)
+        ).astype(bf16)
+        k_aug[1, rows, :] = jnp.where(
+            lanes >= HEAD_DIM, key, jnp.where(lanes == 0, left_out, 0.0)
+        ).astype(bf16)
+        v_mask[0, rows, :] = jnp.where(lanes < HEAD_DIM, value, 0.0).astype(bf16)
+        v_mask[1, rows, :] = jnp.where(lanes >= HEAD_DIM, value, 0.0).astype(bf16)
+        k_turned[:, rows] = key.T.astype(bf16)
+        v_turned[:, rows] = value.T.astype(bf16)
+
+    def block_rows(high):
+        block = lax.div(flipped(ctx, 2 * high, 3), 2)
+        return block, pl.ds(pl.multiple_of(block * span * 2, span * 2), span * 2)
+
+    arrivals = ([near_y], [near_pair], passed_pair, passed_y)
+    for high in (0, 1, 3, 2):
+        for copy in arrivals[high]:
+            copy.wait()
+        block, rows = block_rows(high)
+        projected = matmul(tokens[rows, :], w_heads[...])
+        put_query(rows, projected[:, :LANES])
+        position = block * span * 2 + lax.broadcasted_iota(jnp.int32, (span * 2, LANES), 0)
+        put_key_value(
+            rows,
+            projected[:, LANES : 2 * LANES],
+            projected[:, 2 * LANES :],
+            jnp.where(position < length, 0.0, -1e30),
+        )
+    projected = matmul(own_mem[upper], w_heads[:, LANES:])
+    position = lax.broadcasted_iota(jnp.int32, (MEM_PAD, LANES), 0)
+    put_key_value(
+        pl.ds(length_all, MEM_PAD),
+        projected[:, :LANES],
+        projected[:, LANES:],
+        jnp.where(position < MEM_ROWS, 0.0, -1e30),
+    )
+
+    att_copies = []
+    for high in (3, 2, 1, 0):
+        _, rows = block_rows(high)
+        for head in range(2):
+            scores = back_product(k_aug[head], q_aug[head, rows, :])
+            exponent = jnp.exp(scores - jnp.max(scores, axis=0, keepdims=True))
+            total = jnp.sum(exponent, axis=0, keepdims=True)
+            inverse = 1.0 / total
+            inverse_total[head : head + 1, rows] = inverse
+            weights = exponent.astype(bf16)
+            probs[head, :, rows] = weights
+            half = pl.ds(head * HEAD_DIM, HEAD_DIM)
+            mixed_t[half, rows] = matmul(v_turned[half, :], weights) * inverse
+        mixed[rows, :] = mixed_t[:, rows].T.astype(bf16)
+        att_items = []
+        for low in (0, 1):
+            offset = 2 * high + low
+            source = mixed.at[span_rows(flipped(ctx, offset, 3))]
+            target = att.at[span_rows(upper), pair_lanes(pair)]
+            if offset:
+                att_items.append((source, target, ctx_peer(offset)))
+            else:
+                own_att = copies.keep([(source, target)], source)
+
+        att_copies.append(copies.send_all(att_items, mixed.at[pl.ds(0, span * len(att_items))]))
+
+    y_down.wait()
+    x_up.wait()
+    places = (
+        rows_of(w_up, x_owner),
+        rows_of(w_down, x_owner, (1 - y_side) * half_down, half_down),
+    )
+    passed_weights = copies.send_all(
+        [(place, place, shard_peer(1)) for place in places],
+        partial.at[0, pl.ds(0, half_down + width)],
+    )
+    for block in range(4):
+        rows = pl.ds(block * span * 2, span * 2)
+        tokens_t[:, rows] = tokens[rows, :].astype(f32).T.astype(bf16)
+    core_weights.wait()
+    passed_early.wait()
+    passed_weights.wait()
+    own_att.wait()
+    for copy in att_copies:
+        copy.wait()
+
+    seqs = own_in.shape[0]
+    local_rows = seqs * span
+    own_x = own_in[...].reshape(local_rows, width).astype(f32)
+    branch = matmul(att[...], w_out[...]) + full_vec(2)
+    normed, unit_one, inverse_one = norm_forward(own_x + branch, full_vec(4), full_vec(5))
+    normed_low = normed.astype(bf16)
+    ffn_out = jnp.zeros((local_rows, width), f32)
+    for chunk in range(4):
+        columns = pl.ds(chunk * width, width)
+        bias = jnp.concatenate([vecs[chunk, 8 + i : 9 + i, :] for i in range(4)], axis=1)
+        pre_act = matmul(normed_low, w_up[:, columns]) + bias
+        square = pre_act * pre_act
+        bent = jnp.tanh(GELU_SCALE * pre_act * (1.0 + 0.044715 * square))
+        hidden[:, columns] = (0.5 * pre_act * (1.0 + bent)).astype(bf16)
+        act_slope[:, columns] = 0.5 * (1.0 + bent) + 0.5 * pre_act * (1.0 - bent * bent) * (
+            GELU_SCALE * (1.0 + 3 * 0.044715 * square)
+        )
+        ffn_out = ffn_out + matmul(hidden[:, columns], w_down[columns, :])
+    ffn_out = ffn_out + full_vec(3)
+    output, unit_two, inverse_two = norm_forward(normed + ffn_out, full_vec(6), full_vec(7))
+    out_rows[...] = output.astype(bf16)
+
+    chunks = []
+    first_row = 0
+    for rows, order in PIECES:
+        chunks.append((first_row, rows, order))
+        first_row += rows
+    sides = {"x": x_half, "y": y_side, "z": z_side}
+    peers = {"x": shard_peer(2), "y": ctx_peer(1), "z": ctx_peer(2)}
+    waits = {}
+    out_copies = [copies.keep([(out_rows, o_layer)], out_rows)]
+    final_items, input_items = [], []
+
+    def arrived(key):
+        waits.pop(key).wait()
+
+    def add_rows(target, first):
+        target[...] = (target[...].astype(f32) + first[...].astype(f32)).astype(bf16)
+
+    def aligned(start, rows):
+        return pl.ds(pl.multiple_of(start, rows), rows)
+
+    def core_send(number):
+        start, rows, _ = chunks[number]
+        waits["core", number] = copies.send_all(
+            [
+                (
+                    partial.at[2 * side + 1 - core, pl.ds(start, rows)],
+                    got_core.at[side, pl.ds(start, rows)],
+                    shard_peer(1),
+                )
+                for side in range(2)
+            ],
+            partial.at[0, pl.ds(0, 2 * rows)],
+        )
+
+    def slabs(number, step):
+        start, rows, order = chunks[number]
+        if step == 0:
+            return [got_core.at[side, pl.ds(start, rows)] for side in range(2)]
+        buffer = (got_first, got_second, got_third)[step - 1]
+        size = rows >> (step - 1)
+        first = start >> (step - 1)
+        if "x" in order[:step]:
+            return [buffer.at[pl.ds(first, size)]]
+        return [buffer.at[pl.ds(first + side * (size // 2), size // 2)] for side in range(2)]
+
+    def split(number, step):
+        whole = slabs(number, step)
+        axis = chunks[number][2][step]
+        side = sides[axis]
+        if axis == "x":
+            start, rows, _ = chunks[number]
+            if step == 0:
+                return (
+                    [got_core.at[side, pl.ds(start, rows)]],
+                    [got_core.at[1 - side, pl.ds(start, rows)]],
+                )
+            buffer = (got_first, got_second, got_third)[step - 1]
+            size, first = rows >> step, start >> (step - 1)
+            return (
+                [buffer.at[aligned(first + side * size, size)]],
+                [buffer.at[aligned(first + (1 - side) * size, size)]],
+            )
+        half = whole[0].shape[0] // 2
+        return (
+            [slab.at[aligned(side * half, half)] for slab in whole],
+            [slab.at[aligned((1 - side) * half, half)] for slab in whole],
+        )
+
+    def halve(number, step):
+        if step == 0:
+            arrived(("core", number))
+            for side, slab in enumerate(slabs(number, 0)):
+                start, rows, _ = chunks[number]
+                add_rows(slab, partial.at[2 * side + core, pl.ds(start, rows)])
+        else:
+            join(number, step)
+        axis = chunks[number][2][step]
+        _, gone = split(number, step)
+        start, rows, _ = chunks[number]
+        waits[step, number] = copies.send_all(
+            [(slab, target, peers[axis]) for slab, target in zip(gone, slabs(number, step + 1))],
+            (got_first, got_second, got_third)[step].at[pl.ds(start >> step, rows >> step)],
+        )
+
+    def join(number, step):
+        arrived((step - 1, number))
+        kept, _ = split(number, step - 1)
+        for target, slab in zip(slabs(number, step), kept):
+            add_rows(target, slab)
+
+    def cross(number):
+        join(number, 3)
+        start, rows, _ = chunks[number]
+        here = pl.ds(start // 4, rows // 4)
+        waits["cross", number] = copies.send(got_third.at[here], got_far.at[here], ctx_peer(6))
+
+    def place_of(number, count):
+        start, rows, order = chunks[number]
+        for axis in order.replace("x", "")[: 2 - count]:
+            rows = rows // 2
+            start = start + sides[axis] * rows
+        return aligned(start, rows)
+
+    def gather(number, count):
+        start, rows, order = chunks[number]
+        if count == 0:
+            arrived(("cross", number))
+            here = pl.ds(start // 4, rows // 4)
+            final[place_of(number, 0), :] = (
+                got_third[here, :].astype(f32) + got_far[here, :].astype(f32)
+            ).astype(bf16)
+        else:
+            arrived(("gather", number))
+        place = final.at[place_of(number, count)]
+        waits["gather", number] = copies.send(
+            place, place, peers[order.replace("x", "")[1 - count]]
+        )
+
+    def write_out(number):
+        start, rows, _ = chunks[number]
+        arrived(("gather", number))
+        place = pl.ds(start, rows)
+        final_items.append((final.at[place], o_fin.at[place]))
+        if len(final_items) == len(chunks):
+            out_copies.append(copies.keep(final_items, final))
+
+    def outer_part(number):
+        start, rows, _ = chunks[number]
+        done = 0
+        while done < rows:
+            row = start + done
+            if row < width:
+                size = min(rows - done, width - row)
+                for owner in range(4):
+                    columns = slice(owner * width + row, owner * width + row + size)
+                    partial[owner, row : row + size, :] = outer_sum(
+                        hidden[:, columns], held.d_ffn
+                    ).astype(bf16)
+            else:
+                size = LANES
+                if row < 2 * width:
+                    chunk = (row - width) // LANES
+                    grad = outer_sum(
+                        held.normed, d_pre[:, chunk * width : (chunk + 1) * width]
+                    ).astype(bf16)
+                else:
+                    grad = outer_sum(att[...], d_branch[...]).astype(bf16)
+                for owner in range(4):
+                    partial[owner, row : row + size, :] = grad[owner * LANES : (owner + 1) * LANES]
+            done += size
+        core_send(number)
+
+    held = Held()
+    held.normed = normed_low
+
+
+    def second_norm():
+        cotangent = own_g[...].reshape(local_rows, width).astype(f32)
+        held.two, held.second_gain, held.second_bias = norm_backward(
+            cotangent, unit_two, inverse_two, full_vec(6)
+        )
+        held.d_ffn = held.two.astype(bf16)
+
+    def first_norm():
+        d_normed = held.two
+        for chunk in range(4):
+            columns = pl.ds(chunk * width, width)
+            d_hidden = back_product(held.d_ffn, w_down[columns, :])
+            d_chunk = (d_hidden * act_slope[:, columns]).astype(bf16)
+            d_pre[:, columns] = d_chunk
+            d_normed = d_normed + back_product(d_chunk, w_up[:, columns])
+        d_one, held.first_gain, held.first_bias = norm_backward(
+            d_normed, unit_one, inverse_one, full_vec(4)
+        )
+        in_grad[...] = d_one
+        d_branch[...] = d_one.astype(bf16)
+
+    def attended_grad():
+        held.d_att = []
+        for rows_of_seq, offsets in ((1 - upper, (6, 7, 4, 5)), (upper, (2, 3, 1, 0))):
+            rows = span_rows(rows_of_seq)
+            d_att[rows, :] = back_product(d_branch[rows, :], w_out[...]).astype(bf16)
+            items = []
+            for offset in offsets:
+                peer = flipped(ctx, offset, 3)
+                source = d_att.at[rows, pair_lanes(lax.rem(peer, 4))]
+                target = d_mixed.at[span_rows(ctx)]
+                if offset:
+                    items.append((source, target, ctx_peer(offset)))
+                else:
+                    held.own_d_att = copies.keep([(source, target)], target)
+            held.d_att.append(copies.send_all(items, d_mixed.at[pl.ds(0, span * len(items))]))
+
+    def square_sums():
+        row_id = lax.broadcasted_iota(jnp.int32, (8, LANES), 0)
+        tile = jnp.zeros((8, LANES), f32)
+        for seq in range(seqs):
+            position = ctx * span + lax.broadcasted_iota(jnp.int32, (span, 1), 0)
+            valid = jnp.where(position < len_ref[seq], 1.0, 0.0)
+            for kind, values in enumerate((own_x, branch, ffn_out)):
+                piece = values[seq * span : (seq + 1) * span]
+                row_sum = jnp.sum(piece * piece, axis=1, keepdims=True) * valid
+                tile = tile + jnp.where(
+                    row_id == seq * 3 + kind, jnp.sum(row_sum, axis=0, keepdims=True), 0.0
+                )
+        squares[ctx] = tile
+        held.squares = copies.send_all(
+            [
+                (squares.at[ctx], squares.at[ctx], ctx_peer(offset))
+                for offset in (6, 7, 4, 5, 2, 3, 1)
+            ],
+            squares.at[pl.ds(0, 7)],
+        )
+
+    def narrow_grads():
+        vec_part[...] = jnp.zeros_like(vec_part)
+        wide_grads = (
+            jnp.sum(d_branch[...].astype(f32), axis=0, keepdims=True),
+            jnp.sum(held.d_ffn.astype(f32), axis=0, keepdims=True),
+            held.first_gain,
+            held.first_bias,
+            held.second_gain,
+            held.second_bias,
+        )
+        for owner in range(4):
+            for kind, values in enumerate(wide_grads):
+                vec_part[owner, 2 + kind : 3 + kind, :] = values.reshape(1, width)[
+                    :, owner * LANES : (owner + 1) * LANES
+                ]
+            columns = pl.ds(owner * width, width)
+            bias = jnp.sum(d_pre[:, columns].astype(f32), axis=0, keepdims=True)
+            for part in range(4):
+                vec_part[owner, 8 + part : 9 + part, :] = bias[
+                    :, part * LANES : (part + 1) * LANES
+                ]
+
+    def deltas():
+        held.own_d_att.wait()
+        for copy in held.d_att:
+            copy.wait()
+        turned = d_mixed[...].astype(f32).T
+        products = turned * mixed_t[...]
+        held.deltas = []
+        for head in range(2):
+            half = slice(head * HEAD_DIM, (head + 1) * HEAD_DIM)
+            inverse = inverse_total[head : head + 1, :]
+            held.deltas.append(jnp.sum(products[half], axis=0, keepdims=True) * inverse)
+            d_scaled_t[half, :] = (turned[half] * inverse).astype(bf16)
+        d_scaled[...] = d_scaled_t[...].astype(f32).T.astype(bf16)
+
+    def score_grads(head):
+        delta = held.deltas[head]
+        for block in range(4):
+            rows = slice(block * span * 2, (block + 1) * span * 2)
+            dots = matmul(v_mask[head], d_scaled_t[:, rows])
+            weights = probs[head, :, rows].astype(f32)
+            d_scores[head, :, rows] = (weights * (dots - delta[:, rows])).astype(bf16)
+
+    def scores_0():
+        score_grads(0)
+
+    def scores_1():
+        score_grads(1)
+
+    def key_value_grads():
+        key_lane = lax.broadcasted_iota(jnp.int32, (keys, LANES), 1)
+        grad_value = jnp.where(
+            key_lane < HEAD_DIM, matmul(probs[0], d_scaled[...]), matmul(probs[1], d_scaled[...])
+        ).astype(bf16)
+        grad_key = jnp.where(
+            key_lane < HEAD_DIM,
+            matmul(d_scores[0], q_scaled[...]),
+            matmul(d_scores[1], q_scaled[...]),
+        ).astype(bf16)
+        joined[:, LANES : 2 * LANES] = grad_key[:length_all]
+        joined[:, 2 * LANES :] = grad_value[:length_all]
+        held.memory = jnp.concatenate([grad_key[length_all:], grad_value[length_all:]], axis=1)
+        held.value = jnp.sum(grad_value.astype(f32), axis=0, keepdims=True)
+
+    def query_grads():
+        grad_query = jnp.concatenate(
+            [
+                matmul(k_turned[:HEAD_DIM, :], d_scores[0]),
+                matmul(k_turned[HEAD_DIM:, :], d_scores[1]),
+            ],
+            axis=0,
+        ) * (HEAD_DIM**-0.5)
+        grad_query = grad_query.T.astype(bf16)
+        joined[:, :LANES] = grad_query
+        held.query = jnp.sum(grad_query.astype(f32), axis=0, keepdims=True)
+
+    def input_part(mirror, order):
+        for place, offset in enumerate(order):
+            rows = span_rows(flipped(ctx, offset ^ mirror, 3))
+            dx_part[
+                4 * (mirror == 0) + place
+            ] = back_product(joined[rows, :], w_heads[...]).astype(bf16)
+
+    def two(ref, first):
+        return ref.at[pl.ds(first, 2)]
+
+    def input_far():
+        input_part(6, (0, 2, 1, 3))
+        held.far_y = copies.send(two(dx_part, 2), two(dx_got, 0), ctx_peer(1))
+
+    def input_near():
+        input_part(0, (0, 2, 1, 3))
+        held.near_y = copies.send(two(dx_part, 6), two(dx_got, 2), ctx_peer(1))
+
+    def input_far_z():
+        held.far_y.wait()
+        add_rows(two(dx_part, 0), two(dx_got, 0))
+        held.far_z = copies.send(dx_part.at[1], dx_got.at[4], ctx_peer(2))
+
+    def input_near_z():
+        held.near_y.wait()
+        add_rows(two(dx_part, 4), two(dx_got, 2))
+        held.near_z = copies.send(dx_part.at[5], dx_got.at[5], ctx_peer(2))
+
+    def input_cross():
+        held.far_z.wait()
+        add_rows(dx_got.at[4], dx_part.at[0])
+        held.cross = copies.send(dx_got.at[4], dx_far, ctx_peer(6))
+
+    def write_input_rows(index, parts):
+        rows = span_rows(index)
+        total = in_grad[rows, :]
+        for part in parts:
+            total = total + part.astype(f32)
+        in_grad[rows, :] = total
+        input_items.append((in_grad.at[rows], o_input.at[rows]))
+        if len(input_items) == 2:
+            out_copies.append(copies.keep(input_items, in_grad))
+
+    def input_near_out():
+        held.near_z.wait()
+        write_input_rows(upper, (dx_part[4], dx_got[5]))
+
+    def input_far_out():
+        held.cross.wait()
+        write_input_rows(1 - upper, (dx_far[...],))
+
+    def memory_part():
+        mem_part[pair] = back_product(held.memory, w_heads[:, LANES:]).astype(bf16)
+        held.mem = copies.send_all(
+            [(mem_part.at[pair], mem_part.at[pair], ctx_peer(offset)) for offset in (3, 2, 1)],
+            mem_part.at[pl.ds(0, 3)],
+        )
+
+    def memory_cross():
+        held.mem.wait()
+        mem_far[upper] = (
+            mem_part[0].astype(f32)
+            + mem_part[1].astype(f32)
+            + mem_part[2].astype(f32)
+            + mem_part[3].astype(f32)
+        ).astype(bf16)
+        held.mem_far = copies.send(mem_far.at[upper], mem_far.at[upper], ctx_peer(6))
+
+    def memory_out():
+        held.mem_far.wait()
+        out_copies.append(copies.keep([(mem_far, o_mem)], mem_far))
+
+    def head_grads():
+        grad_heads = matmul(tokens_t[...], joined[...])
+        mem_grad = outer_sum(own_mem[upper], held.memory)
+        for owner in range(4):
+            rows = slice(owner * LANES, (owner + 1) * LANES)
+            head_part[owner, :LANES, :LANES] = grad_heads[rows, :LANES].astype(bf16)
+            head_part[owner, :LANES, LANES:] = (grad_heads[rows, LANES:] + mem_grad[rows]).astype(
+                bf16
+            )
+            mine = pair == owner
+            vec_part[owner, 0:1, :] = jnp.where(mine, held.query, 0.0)
+            vec_part[owner, 1:2, :] = jnp.where(mine, held.value, 0.0)
+            head_part[owner, LANES:, :] = jnp.zeros((ROW_KINDS, 3 * LANES), bf16)
+            head_part[owner, LANES:, :LANES] = vec_part[owner].astype(bf16)
+        held.head_core = copies.send_all(
+            [
+                (head_part.at[2 * side + 1 - core], head_core.at[side], shard_peer(1))
+                for side in range(2)
+            ],
+            head_core,
+        )
+
+    def head_x_send():
+        held.head_core.wait()
+        for side in range(2):
+            add_rows(head_core.at[side], head_part.at[2 * side + core])
+        held.head_x = copies.send(head_core.at[1 - x_half], head_x, shard_peer(2))
+
+    def head_far_send():
+        held.head_x.wait()
+        add_rows(head_x, head_core.at[x_half])
+        held.head_far = copies.send(head_x, head_far, ctx_peer(4))
+
+    def head_gather():
+        held.head_far.wait()
+        head_all[pair] = (head_x[...].astype(f32) + head_far[...].astype(f32)).astype(bf16)
+        held.heads = copies.send(head_all.at[pair], head_all.at[pair], ctx_peer(2))
+
+    def head_spread():
+        held.heads.wait()
+        places = [head_all.at[index] for index in (pair, flipped(pair, 2, 2))]
+        held.heads = copies.send_all(
+            [(place, place, ctx_peer(1)) for place in places], head_all.at[pl.ds(0, 2)]
+        )
+
+    def head_out():
+        held.heads.wait()
+        out_copies.append(copies.keep([(head_all, o_heads)], head_all))
+
+    def rms_out():
+        held.squares.wait()
+        row_id = lax.broadcasted_iota(jnp.int32, (8, LANES), 0)
+        total = squares[0]
+        for other in range(1, spans):
+            total = total + squares[other]
+        valid_tokens = jnp.where(row_id < 3, len_ref[0], len_ref[1]).astype(f32)
+        rms_rows[...] = jnp.sqrt(total / (valid_tokens * width))
+        out_copies.append(copies.keep([(rms_rows, o_rms)], rms_rows))
+
+    second_norm()
+    outer_part(0)
+    outer_part(1)
+    outer_part(2)
+    outer_part(3)
+    first_norm()
+    attended_grad()
+    outer_part(4)
+    outer_part(5)
+    outer_part(6)
+    square_sums()
+    narrow_grads()
+    halve(0, 0)
+    halve(1, 0)
+    halve(2, 0)
+    halve(3, 0)
+    halve(4, 0)
+    halve(5, 0)
+    halve(0, 1)
+    halve(6, 0)
+    halve(2, 1)
+    deltas()
+    scores_0()
+    halve(1, 1)
+    scores_1()
+    halve(3, 1)
+    key_value_grads()
+    halve(0, 2)
+    halve(4, 1)
+    query_grads()
+    halve(2, 2)
+    input_far()
+    halve(3, 2)
+    halve(5, 1)
+    halve(6, 1)
+    input_near()
+    memory_part()
+    cross(0)
+    head_grads()
+    halve(1, 2)
+    cross(2)
+    cross(3)
+    halve(6, 2)
+    halve(4, 2)
+    gather(0, 0)
+    head_x_send()
+    cross(1)
+    cross(6)
+    gather(2, 0)
+    gather(3, 0)
+    cross(4)
+    gather(0, 1)
+    gather(1, 0)
+    head_far_send()
+    input_far_z()
+    gather(6, 0)
+    gather(2, 1)
+    gather(3, 1)
+    halve(5, 2)
+    gather(4, 0)
+    cross(5)
+    input_cross()
+    head_gather()
+    input_near_z()
+    gather(6, 1)
+    memory_cross()
+    gather(4, 1)
+    write_out(0)
+    gather(1, 1)
+    gather(5, 0)
+    write_out(2)
+    write_out(3)
+    write_out(6)
+    input_far_out()
+    head_spread()
+    write_out(4)
+    gather(5, 1)
+    input_near_out()
+    memory_out()
+    rms_out()
+    write_out(1)
+    head_out()
+    write_out(5)
+    for copy in out_copies:
+        copy.wait()
+    copies.finish()
+    assert (len(copies.sent), copies.received, copies.kept) == (SENDS, ARRIVALS, KEPT)
+
+
+def outputs_kernel(layer, input_grad, mem_grad, weights, heads, rms, *outs):
+    f32 = jnp.float32
+    (
+        o_layer,
+        o_input,
+        o_mem,
+        o_query,
+        o_key,
+        o_value,
+        o_out,
+        o_up,
+        o_down,
+        o_b_query,
+        o_b_value,
+        o_b_out,
+        o_b_up,
+        o_b_down,
+        o_first_gain,
+        o_first_bias,
+        o_second_gain,
+        o_second_bias,
+        o_rms,
+    ) = outs
+    width = weights.shape[1]
+    o_layer[...] = layer[...].reshape(o_layer.shape)
+    o_input[...] = input_grad[...].reshape(o_input.shape)
+    for seq in range(o_mem.shape[1]):
+        o_mem[:, seq, :] = mem_grad[seq].astype(f32)[:MEM_ROWS]
+    o_down[...] = weights[:width, :].astype(f32)
+    for chunk in range(4):
+        o_up[:, chunk * width : (chunk + 1) * width] = weights[
+            width + chunk * LANES : width + (chunk + 1) * LANES, :
+        ].astype(f32)
+    o_out[...] = weights[2 * width :, :].astype(f32)
+    for owner in range(4):
+        for part, ref in enumerate((o_query, o_key, o_value)):
+            ref[:, owner * LANES : (owner + 1) * LANES] = heads[
+                owner, :LANES, part * LANES : (part + 1) * LANES
+            ].astype(f32)
+    vec = (
+        heads[0, LANES:, :LANES].astype(f32)
+        + heads[1, LANES:, :LANES].astype(f32)
+        + heads[2, LANES:, :LANES].astype(f32)
+        + heads[3, LANES:, :LANES].astype(f32)
+    )
+    narrow = (
+        o_b_query,
+        o_b_value,
+        o_b_out,
+        o_b_down,
+        o_first_gain,
+        o_first_bias,
+        o_second_gain,
+        o_second_bias,
+    )
+    for kind, ref in enumerate(narrow):
+        ref[...] = vec[kind]
+    for piece in range(4):
+        o_b_up[piece * LANES : (piece + 1) * LANES] = vec[8 + piece]
+    for seq in range(o_rms.shape[0]):
+        for kind in range(3):
+            o_rms[seq : seq + 1, kind : kind + 1] = rms[seq * 3 + kind : seq * 3 + kind + 1, :1]
+
+
+def fast_layer(
+    inputs,
+    memory,
+    lengths,
+    w_query,
+    w_key,
+    w_value,
+    w_out,
+    w_up,
+    w_down,
+    b_query,
+    b_value,
+    b_out,
+    b_up,
+    b_down,
+    first_gain,
+    first_bias,
+    second_gain,
+    second_bias,
+    out_grad,
+):
+    bf16, f32 = jnp.bfloat16, jnp.float32
+    seqs, span, width = inputs.shape
+    length_all, keys = 8 * span, 8 * span + MEM_PAD
+    hidden_width = w_up.shape[1]
+    narrow = (b_query, b_value, b_out, b_down, first_gain, first_bias, second_gain, second_bias)
+    vmem, anywhere = pl.BlockSpec(memory_space=pltpu.VMEM), pl.BlockSpec(memory_space=pl.ANY)
+    smem = pl.BlockSpec(memory_space=pltpu.SMEM)
+    stacked = 2 * width + LANES
+    scratch = [
+        ((seqs, span, width), bf16),
+        ((seqs, span, width), bf16),
+        ((seqs, MEM_PAD, width), bf16),
+        ((memory.shape[1], seqs, width), bf16),
+        *[(ref.shape, bf16) for ref in (*narrow, b_up)],
+        ((8, LANES), f32),
+        ((seqs * span, width), bf16),
+        ((length_all, 3 * LANES), bf16),
+        ((seqs * span, width), bf16),
+        ((seqs * span, width), f32),
+        ((length_all, width), bf16),
+        ((width, length_all), bf16),
+        ((width, 3 * LANES), bf16),
+        ((width, width), bf16),
+        ((width, hidden_width), bf16),
+        ((hidden_width, width), bf16),
+        ((4, ROW_KINDS, LANES), f32),
+        ((length_all, LANES), bf16),
+        ((2, length_all, LANES), bf16),
+        ((2, keys, LANES), bf16),
+        ((2, keys, LANES), bf16),
+        ((LANES, keys), bf16),
+        ((LANES, keys), bf16),
+        ((2, keys, length_all), bf16),
+        ((2, keys, length_all), bf16),
+        ((LANES, length_all), f32),
+        ((8, length_all), f32),
+        ((length_all, LANES), bf16),
+        ((LANES, length_all), bf16),
+        ((length_all, LANES), bf16),
+        ((seqs * span, width), bf16),
+        ((seqs * span, hidden_width), bf16),
+        ((seqs * span, hidden_width), f32),
+        ((seqs * span, hidden_width), bf16),
+        ((seqs * span, width), bf16),
+        ((length_all, LANES), bf16),
+        ((4, stacked, width), bf16),
+        ((2, stacked, width), bf16),
+        ((stacked, width), bf16),
+        ((stacked // 2, width), bf16),
+        ((stacked // 4, width), bf16),
+        ((stacked // 4, width), bf16),
+        ((stacked, width), bf16),
+        ((4, LANES + ROW_KINDS, 3 * LANES), bf16),
+        ((2, LANES + ROW_KINDS, 3 * LANES), bf16),
+        ((LANES + ROW_KINDS, 3 * LANES), bf16),
+        ((LANES + ROW_KINDS, 3 * LANES), bf16),
+        ((4, LANES + ROW_KINDS, 3 * LANES), bf16),
+        ((4, ROW_KINDS, LANES), f32),
+        ((8, span, width), bf16),
+        ((6, span, width), bf16),
+        ((span, width), bf16),
+        ((4, MEM_PAD, width), bf16),
+        ((2, MEM_PAD, width), bf16),
+        ((8, 8, LANES), f32),
+    ]
+    made = pl.pallas_call(
+        layer_kernel,
+        out_shape=[
+            jax.ShapeDtypeStruct((seqs * span, width), bf16),
+            jax.ShapeDtypeStruct((seqs * span, width), f32),
+            jax.ShapeDtypeStruct((seqs, MEM_PAD, width), bf16),
+            jax.ShapeDtypeStruct((stacked, width), bf16),
+            jax.ShapeDtypeStruct((4, LANES + ROW_KINDS, 3 * LANES), bf16),
+            jax.ShapeDtypeStruct((8, LANES), f32),
+        ],
+        in_specs=[anywhere] * 3 + [smem] + [anywhere] * 15,
+        out_specs=[anywhere] * 6,
+        scratch_shapes=[pltpu.VMEM(shape, kind) for shape, kind in scratch]
+        + [pltpu.SemaphoreType.DMA((count,)) for count in (SENDS, ARRIVALS, KEPT)],
+        compiler_params=pltpu.CompilerParams(
+            collective_id=0, has_side_effects=True, vmem_limit_bytes=60 * 2**20
+        ),
+        name="layer",
+    )(
+        inputs,
+        out_grad,
+        memory.transpose(1, 0, 2),
+        lengths,
+        w_query,
+        w_key,
+        w_value,
+        w_out,
+        w_up,
+        w_down,
+        *narrow,
+        b_up,
+    )
+    mem_rows = memory.shape[1]
+    shapes = (
+        ((seqs, span, width), bf16),
+        ((seqs, span, width), f32),
+        ((mem_rows, seqs, width), f32),
+        (w_query.shape, f32),
+        (w_key.shape, f32),
+        (w_value.shape, f32),
+        (w_out.shape, f32),
+        (w_up.shape, f32),
+        (w_down.shape, f32),
+        (b_query.shape, f32),
+        (b_value.shape, f32),
+        (b_out.shape, f32),
+        (b_up.shape, f32),
+        (b_down.shape, f32),
+        (first_gain.shape, f32),
+        (first_bias.shape, f32),
+        (second_gain.shape, f32),
+        (second_bias.shape, f32),
+        ((seqs, 3), f32),
+    )
+    outs = pl.pallas_call(
+        outputs_kernel,
+        out_shape=[jax.ShapeDtypeStruct(shape, kind) for shape, kind in shapes],
+        in_specs=[vmem] * 6,
+        out_specs=[vmem] * len(shapes),
+        compiler_params=pltpu.CompilerParams(vmem_limit_bytes=60 * 2**20),
+        name="outputs",
+    )(*made)
+    return (*outs[:2], outs[2].transpose(1, 0, 2), *outs[3:])
+
+
+def takes_fast_plan(mesh, inputs, memory, w_up):
+    return (
+        mesh.shape["shard"] == 4
+        and mesh.shape["ctx"] == 8
+        and inputs.shape == (2, LANES, HEADS * HEAD_DIM)
+        and memory.shape[1] == MEM_ROWS
+        and w_up.shape == (LANES, 4 * HEADS * HEAD_DIM)
+    )
+
+
 def solution(mesh):
     in_specs = (
         P("shard", "ctx", None),
@@ -578,4 +1769,10 @@
         P("shard"),
         P("shard", None),
     )
-    return jax.shard_map(local, mesh=mesh, in_specs=in_specs, out_specs=out_specs, check_vma=False)
+
+    def layer(*arrays):
+        if takes_fast_plan(mesh, arrays[0], arrays[1], arrays[7]):
+            return fast_layer(*arrays)
+        return local(*arrays)
+
+    return jax.shard_map(layer, mesh=mesh, in_specs=in_specs, out_specs=out_specs, check_vma=False)

time: 581 us -> 97.1 us (0.17)
  blocking collectives: 324 us -> 0 us
  waiting for transfers between devices: 103 us -> 0 us
  Pallas kernels: 0 us -> 96.1 us
  matrix products: 74.5 us -> 0 us
  local copies, waits for them, and re-layouts: 43.1 us -> 0 us
  between operations: 16.8 us -> 0.83 us
  other arithmetic: 12.6 us -> 0 us
    psum x2 -> x0, blocking collectives: 173 us -> none  [the longest x1 131 us: local(): lax.psum((part_query, part_key, part_value, part_out, part_up, part_down,...]
    all_gather x15 -> x0, blocking collectives: 142 us -> none  [the longest x1 32.4 us: local(): lax.all_gather(log_total, 'ctx', axis=1, tiled=True)]
    pallas_call x0 -> x2, Pallas kernels: none -> 96.1 us  [the longest x1 92.4 us: fast_layer(): pl.pallas_call(layer_kernel, out_shape=[jax.ShapeDtypeStruct((seqs * span...]
    dot_general x36 -> x0, matrix products: 74.5 us -> none  [the longest x8 11.9 us: matmul(): return jnp.dot(operand, second, preferred_element_type=jnp.float32)]
    unnamed x15 -> x0, waiting for transfers between devices: 50.5 us -> none
    all_gather x6 -> x0, waiting for transfers between devices: 38.8 us -> none  [the longest x1 20.4 us: local(): lax.all_gather(w_down, 'shard', axis=0, tiled=True)]
    unnamed x140 -> x0, local copies, waits for them, and re-layouts: 18.1 us -> none
    all_gather x4 -> x0, local copies, waits for them, and re-layouts: 15.5 us -> none  [the longest x1 4.41 us: local(): lax.all_gather(grad_att, 'ctx', axis=1, tiled=True)]
  transfers between devices with their start and end apart: 12 -> 0, of which waited for: 6 -> 0; matrix products, arithmetic and copies ran while one was open for 21% -> 0% of each run, Pallas kernels for 0% -> 0%
where the time goes in v2:
time: 97.1 us; the launch traced here: 96.9 us
  Pallas kernels  96.1 us (99%)
    pallas_call x1, Pallas kernels, fast_layer(): pl.pallas_call(layer_kernel, out_shape=[jax.ShapeDtypeStruct((seqs * span...  92.4 us
    pallas_call x1, Pallas kernels, fast_layer(): pl.pallas_call(outputs_kernel, out_shape=[jax.ShapeDtypeStruct(shape, kin...  3.64 us

profile of v2, /device:TPU:0, one launch (start us, length us, event | category | flops | bytes accessed | tf_op | source)
XLA Modules:
  0.0 96.9 jit_solution(17202569944349072734)
XLA Ops:
  0.7 92.4 %layer.1 = (bf16[256,512]{1,0:T(8,128)(2,1)}, f32[256,512]{1,0:T(8,128)}, bf16[2,32,512]{2,1,0:T(8,128)(2,1)}, bf16[1152,512]{1,0:T(8,128)(2,1)}, bf16[4,144,384]{2,1,0:T(8,128)(2,1)}, /*index=5*/f32[8,128]{1,0:T(8,128)}) custom-call(bf16[2,128,512]{2,1,0:T(8,128)(2,1)} %x_ref.1, bf16[2,128,512]{2,1,0:T(8,128)(2,1)} %g_ref.1, bf16[20,2,512]{2,1,0:T(2,128)(2,1)} %bitcast.2, ...), custom_call_target="tpu_custom_call" | custom-call | tf_op jit(solution)/shard_map/layer/pallas_call | solution.py:1654
  93.1 3.6 %outputs.1 = (bf16[2,128,512]{2,1,0:T(8,128)(2,1)}, f32[2,128,512]{2,1,0:T(8,128)}, f32[20,2,512]{2,1,0:T(2,128)}, f32[128,512]{1,0:T(8,128)}, f32[128,512]{1,0:...) custom-call(bf16[256,512]{1,0:T(8,128)(2,1)} %get-tuple-element.44.l, ...), custom_call_target="tpu_custom_call" | custom-call | tf_op jit(solution)/shard_map/outputs/pallas_call | solution.py:1708

commit v3 on v2

--- a/solution.py
+++ b/solution.py
@@ -543,7 +543,7 @@
 LANES = 128
 MEM_PAD = 32
 ROW_KINDS = 16
-SENDS, ARRIVALS, KEPT = 18, 87, 23
+SENDS, ARRIVALS, KEPT = 18, 89, 23
 PIECES = ((128, 'xyz'), (128, 'zyx'), (128, 'yxz'), (128, 'yxz'), (256, 'xyz'), (256, 'zyx'), (128, 'yzx'))
 
 
@@ -734,6 +734,9 @@
     for offset in range(1, 8):
         pl.semaphore_signal(barrier, inc=1, device_id=ctx_peer(offset), device_id_type=MESH_ID)
 
+    def aligned_rows(index, rows):
+        return pl.ds(pl.multiple_of(index * rows, rows), rows)
+
     def rows_of(ref, index, start=0, rows=None):
         owned = ref.shape[0] // 4
         return ref.at[pl.ds(pl.multiple_of(index * owned + start, LANES), rows or owned)]
@@ -825,7 +828,15 @@
         rows_of(w_down, shard, y_side * half_down, half_down),
         shard_peer(2),
     )
-    x_up = copies.send(wu_ref, rows_of(w_up, shard), shard_peer(2))
+    half_up = wu_ref.shape[0] // 2
+    x_up = [
+        copies.send(
+            wu_ref.at[pl.ds(half * half_up, half_up)],
+            w_up.at[aligned_rows(shard * 2 + half, half_up)],
+            shard_peer(2),
+        )
+        for half in range(2)
+    ]
     core_weights = copies.send_all(
         [(ref, rows_of(full, shard), shard_peer(1)) for ref, full in full_weights], partial.at[0]
     )
@@ -924,6 +935,10 @@
 
     att_copies = []
     for high in (3, 2, 1, 0):
+        if high == 1:
+            x_up[0].wait()
+            place = w_up.at[aligned_rows(x_owner * 2, half_up)]
+            passed_up = copies.send(place, place, shard_peer(1))
         _, rows = block_rows(high)
         for head in range(2):
             scores = back_product(k_aug[head], q_aug[head, rows, :])
@@ -949,21 +964,20 @@
         att_copies.append(copies.send_all(att_items, mixed.at[pl.ds(0, span * len(att_items))]))
 
     y_down.wait()
-    x_up.wait()
+    x_up[1].wait()
     places = (
-        rows_of(w_up, x_owner),
+        w_up.at[aligned_rows(x_owner * 2 + 1, half_up)],
         rows_of(w_down, x_owner, (1 - y_side) * half_down, half_down),
     )
     passed_weights = copies.send_all(
         [(place, place, shard_peer(1)) for place in places],
-        partial.at[0, pl.ds(0, half_down + width)],
+        partial.at[0, pl.ds(0, half_down + 4 * half_up)],
     )
     for block in range(4):
         rows = pl.ds(block * span * 2, span * 2)
         tokens_t[:, rows] = tokens[rows, :].astype(f32).T.astype(bf16)
     core_weights.wait()
     passed_early.wait()
-    passed_weights.wait()
     own_att.wait()
     for copy in att_copies:
         copy.wait()
@@ -974,6 +988,8 @@
     branch = matmul(att[...], w_out[...]) + full_vec(2)
     normed, unit_one, inverse_one = norm_forward(own_x + branch, full_vec(4), full_vec(5))
     normed_low = normed.astype(bf16)
+    passed_up.wait()
+    passed_weights.wait()
     ffn_out = jnp.zeros((local_rows, width), f32)
     for chunk in range(4):
         columns = pl.ds(chunk * width, width)

time: 97.1 us -> 96.4 us (level)
  no operation moved by 1% of the time
where the time goes in v3:
time: 96.4 us; the launch traced here: 96.2 us
  Pallas kernels  95.4 us (99%)
    pallas_call x1, Pallas kernels, fast_layer(): pl.pallas_call(layer_kernel, out_shape=[jax.ShapeDtypeStruct((seqs * span...  91.7 us
    pallas_call x1, Pallas kernels, fast_layer(): pl.pallas_call(outputs_kernel, out_shape=[jax.ShapeDtypeStruct(shape, kin...  3.64 us

profile of v3, /device:TPU:0, one launch (start us, length us, event | category | flops | bytes accessed | tf_op | source)
XLA Modules:
  0.0 96.2 jit_solution(12351523531019343517)
XLA Ops:
  0.7 91.7 %layer.1 = (bf16[256,512]{1,0:T(8,128)(2,1)}, f32[256,512]{1,0:T(8,128)}, bf16[2,32,512]{2,1,0:T(8,128)(2,1)}, bf16[1152,512]{1,0:T(8,128)(2,1)}, bf16[4,144,384]{2,1,0:T(8,128)(2,1)}, /*index=5*/f32[8,128]{1,0:T(8,128)}) custom-call(bf16[2,128,512]{2,1,0:T(8,128)(2,1)} %x_ref.1, bf16[2,128,512]{2,1,0:T(8,128)(2,1)} %g_ref.1, bf16[20,2,512]{2,1,0:T(2,128)(2,1)} %bitcast.2, ...), custom_call_target="tpu_custom_call" | custom-call | tf_op jit(solution)/shard_map/layer/pallas_call | solution.py:1670
  92.4 3.6 %outputs.1 = (bf16[2,128,512]{2,1,0:T(8,128)(2,1)}, f32[2,128,512]{2,1,0:T(8,128)}, f32[20,2,512]{2,1,0:T(2,128)}, f32[128,512]{1,0:T(8,128)}, f32[128,512]{1,0:...) custom-call(bf16[256,512]{1,0:T(8,128)(2,1)} %get-tuple-element.44.l, ...), custom_call_target="tpu_custom_call" | custom-call | tf_op jit(solution)/shard_map/outputs/pallas_call | solution.py:1724

commit v4 on v3

--- a/solution.py
+++ b/solution.py
@@ -1015,7 +1015,8 @@
     peers = {"x": shard_peer(2), "y": ctx_peer(1), "z": ctx_peer(2)}
     waits = {}
     out_copies = [copies.keep([(out_rows, o_layer)], out_rows)]
-    final_items, input_items = [], []
+    final_out, input_out = copies.keep([], final), copies.keep([], in_grad)
+    out_copies += [final_out, input_out]
 
     def arrived(key):
         waits.pop(key).wait()
@@ -1128,9 +1129,7 @@
         start, rows, _ = chunks[number]
         arrived(("gather", number))
         place = pl.ds(start, rows)
-        final_items.append((final.at[place], o_fin.at[place]))
-        if len(final_items) == len(chunks):
-            out_copies.append(copies.keep(final_items, final))
+        pltpu.make_async_copy(final.at[place], o_fin.at[place], final_out.semaphore).start()
 
     def outer_part(number):
         start, rows, _ = chunks[number]
@@ -1336,9 +1335,7 @@
         for part in parts:
             total = total + part.astype(f32)
         in_grad[rows, :] = total
-        input_items.append((in_grad.at[rows], o_input.at[rows]))
-        if len(input_items) == 2:
-            out_copies.append(copies.keep(input_items, in_grad))
+        pltpu.make_async_copy(in_grad.at[rows], o_input.at[rows], input_out.semaphore).start()
 
     def input_near_out():
         held.near_z.wait()

time: 96.4 us -> 96 us (level)
  no operation moved by 1% of the time
where the time goes in v4:
time: 96 us; the launch traced here: 95.9 us
  Pallas kernels  95.1 us (99%)
    pallas_call x1, Pallas kernels, fast_layer(): pl.pallas_call(layer_kernel, out_shape=[jax.ShapeDtypeStruct((seqs * span...  91.4 us
    pallas_call x1, Pallas kernels, fast_layer(): pl.pallas_call(outputs_kernel, out_shape=[jax.ShapeDtypeStruct(shape, kin...  3.64 us

profile of v4, /device:TPU:0, one launch (start us, length us, event | category | flops | bytes accessed | tf_op | source)
XLA Modules:
  0.0 95.9 jit_solution(15177285312164324025)
XLA Ops:
  0.7 91.4 %layer.1 = (bf16[256,512]{1,0:T(8,128)(2,1)}, f32[256,512]{1,0:T(8,128)}, bf16[2,32,512]{2,1,0:T(8,128)(2,1)}, bf16[1152,512]{1,0:T(8,128)(2,1)}, bf16[4,144,384]{2,1,0:T(8,128)(2,1)}, /*index=5*/f32[8,128]{1,0:T(8,128)}) custom-call(bf16[2,128,512]{2,1,0:T(8,128)(2,1)} %x_ref.1, bf16[2,128,512]{2,1,0:T(8,128)(2,1)} %g_ref.1, bf16[20,2,512]{2,1,0:T(2,128)(2,1)} %bitcast.2, ...), custom_call_target="tpu_custom_call" | custom-call | tf_op jit(solution)/shard_map/layer/pallas_call | solution.py:1667
  92.1 3.6 %outputs.1 = (bf16[2,128,512]{2,1,0:T(8,128)(2,1)}, f32[2,128,512]{2,1,0:T(8,128)}, f32[20,2,512]{2,1,0:T(2,128)}, f32[128,512]{1,0:T(8,128)}, f32[128,512]{1,0:...) custom-call(bf16[256,512]{1,0:T(8,128)(2,1)} %get-tuple-element.44.l, ...), custom_call_target="tpu_custom_call" | custom-call | tf_op jit(solution)/shard_map/outputs/pallas_call | solution.py:1721
